TPU v7x, 512 devices: a whole 4x4x16 slice. The times are simulated.
512 devices in a mesh: expert: 8 (over z_lo, core), dp: 64 (over z_hi, x, y).
Axes of the slice: x: 4, y: 4, z: 16 (z_hi: 4, z_lo: 4; z = z_hi * 4 + z_lo), core: 2. Of those that a mesh axis runs over, the one named last changes fastest.
Arguments:
- out_grad: bfloat16 [4096, 3072], P(('expert', 'dp')), may hold values from -6 to 6
- gate_saved: bfloat16 [4096, 2, 8192], P('expert', None, 'dp'), may hold values from -6 to 6
- up_saved: bfloat16 [4096, 2, 8192], P('expert', None, 'dp'), may hold values from -6 to 6
- routing: int32 [4096, 2], P('expert'), may hold values from 0 to 7, all different within a row; in each aligned block of 512 rows (0 to 511, 512 to 1023, ...) at most 256 rows name the same one
- down_weight: bfloat16 [8, 3072, 8192], P('expert', None, 'dp'), may hold values from -0.0625 to 0.0625
- momentum: bfloat16 [8, 3072, 8192], P('expert', 'dp'), may hold values from -60 to 60
Outputs:
- d_gate: bfloat16 [4096, 2, 8192], P('expert', None, 'dp')
- d_up: bfloat16 [4096, 2, 8192], P('expert', None, 'dp')
- new_weight: float32 [8, 3072, 8192], P('expert', 'dp')
- new_momentum: bfloat16 [8, 3072, 8192], P('expert', 'dp')
Inputs may be any that keep to these rules, and one draw needn't show every extreme that they name: `routing`: in each aligned block of 512 tokens (one group), the 2 experts of a token differ, no expert is named by more than 256 tokens, a bound that some block reaches.
All inputs are finite; a program needn't handle non-finite values.
Results may differ from a plain program's by a relative error of at most 0.0015.
Values may be sent and summed in bfloat16 or wider, within the bound.
A program may use at most 128 MiB of HBM per device.

v0:
```python
import jax
import jax.numpy as jnp
from jax import lax
from jax.sharding import PartitionSpec as P

beta_first = 0.9
beta_second = 0.99
step_rate = 0.01
decay_rate = 1.0
sign_width = 10.0


def shifted(array, axis, by):
    size = lax.axis_size(axis)
    return lax.ppermute(array, axis, [(i, (i + by) % size) for i in range(size)])


def slot_table(flat_route, experts, capacity):
    count_rows = flat_route.shape[0]
    onehot = (flat_route[:, None] == jnp.arange(experts, dtype=jnp.int32)[None, :]).astype(
        jnp.int32
    )
    before = jnp.cumsum(onehot, axis=0) - onehot
    place = jnp.sum(before * onehot, axis=1)
    table = jnp.full((experts, capacity), count_rows, jnp.int32)
    table = table.at[flat_route, place].set(jnp.arange(count_rows, dtype=jnp.int32))
    return (table, jnp.sum(onehot, axis=0))


def body(out_grad, gate_saved, up_saved, routing, down_weight, momentum):
    grads_all = lax.all_gather(out_grad, "dp", axis=0, tiled=True)
    group_tok, topk, cols = gate_saved.shape
    count_rows = group_tok * topk
    width = grads_all.shape[1]
    experts = lax.axis_size("expert")
    capacity = min(group_tok, 2 * count_rows // experts)
    gate_rows = gate_saved.reshape(count_rows, cols).astype(jnp.float32)
    up_rows = up_saved.reshape(count_rows, cols).astype(jnp.float32)
    sigma = jax.nn.sigmoid(gate_rows)
    hidden = (gate_rows * sigma * up_rows).astype(jnp.bfloat16)
    hidden_pad = jnp.concatenate([hidden, jnp.zeros((1, cols), jnp.bfloat16)], axis=0)
    grads_pad = jnp.concatenate([grads_all, jnp.zeros((1, width), jnp.bfloat16)], axis=0)
    table, counts = slot_table(routing.reshape(count_rows), experts, capacity)
    mine = lax.axis_index("expert")
    weight_now = down_weight[0]
    carried = jnp.zeros((width, cols), jnp.bfloat16)
    deriv = jnp.zeros((count_rows + 1, cols), jnp.float32)
    for step in range(experts):
        process_deriv = deriv
        slots = table[(mine - step) % experts]
        block_deriv = process_deriv
        upstream = grads_pad[slots // topk]
        picked = hidden_pad[slots]
        block_deriv = block_deriv.at[slots].set(
            jnp.dot(upstream, weight_now, preferred_element_type=jnp.float32)
        )
        total = lax.dot_general(
            upstream, picked, (((0,), (0,)), ((), ())), preferred_element_type=jnp.float32
        )
        process_deriv = block_deriv
        carried, deriv = ((carried.astype(jnp.float32) + total).astype(jnp.bfloat16), process_deriv)
        if step + 1 < experts:
            weight_now, carried = shifted((weight_now, carried), "expert", 1)
        else:
            carried = shifted(carried, "expert", 1)
    dh_rows = deriv[:count_rows]
    d_up = (dh_rows * gate_rows * sigma).astype(jnp.bfloat16).reshape(group_tok, topk, cols)
    d_gate = (
        (dh_rows * up_rows * sigma * (1.0 + gate_rows * (1.0 - sigma)))
        .astype(jnp.bfloat16)
        .reshape(group_tok, topk, cols)
    )
    shard_grad, shard_weight = (
        lax.all_to_all(carried[None], "dp", split_axis=1, concat_axis=2, tiled=True),
        lax.all_to_all(down_weight, "dp", split_axis=1, concat_axis=2, tiled=True),
    )
    grad = shard_grad.astype(jnp.float32)
    moment = momentum.astype(jnp.float32)
    mix = beta_first * moment + (1.0 - beta_first) * grad
    new_weight = shard_weight.astype(jnp.float32) * (
        1.0 - step_rate * decay_rate
    ) - step_rate * jnp.tanh(mix / sign_width)
    new_momentum = (beta_second * moment + (1.0 - beta_second) * grad).astype(jnp.bfloat16)
    return (d_gate, d_up, new_weight, new_momentum)


def solution(mesh):
    placed = (
        P(("expert", "dp"), None),
        P("expert", None, "dp"),
        P("expert", None, "dp"),
        P("expert", None),
        P("expert", None, "dp"),
        P("expert", "dp", None),
    )
    return jax.shard_map(
        body,
        mesh=mesh,
        in_specs=placed,
        out_specs=(
            P("expert", None, "dp"),
            P("expert", None, "dp"),
            P("expert", "dp", None),
            P("expert", "dp", None),
        ),
        check_vma=False,
    )
```

profile of v0, /device:TPU:96, one launch (start us, length us, event | category | flops | bytes accessed | tf_op | source)
XLA Modules:
  0.0 508.0 jit_solution(13077218628343573920)
XLA Ops:
  7.9 1.9 collective-permute-start
  9.9 11.6 %collective-permute-done = bf16[3072,128]{1,0:T(8,128)(2,1)S(1)} collective-permute-done((bf16[3072,128]{1,0:T(8,128)(2,1)}, bf16[3072,128]{1,0:T(8,128)(2,1)S(1)}, u32[]{:S(2)}, u32[]{:S(2)}) %collective-permute-start) | collective-permute-done | bytes 786464 | tf_op jit(solution)/shard_map/ppermute | solution.py:15
  21.4 4.2 collective-permute-start.1
  25.7 9.1 %collective-permute-done.1 = bf16[3072,128]{1,0:T(8,128)(2,1)S(1)} collective-permute-done((bf16[3072,128]{1,0:T(8,128)(2,1)S(1)}, bf16[3072,128]{1,0:T(8,128)(2,1)S(1)}, u32[]{:S(2)}, u32[]{:S(2)}) %collective-permute-start.1) | collective-permute-done | bytes 786464 | tf_op jit(solution)/shard_map/ppermute | solution.py:15
  34.7 6.5 %collective-permute-start.2 = (bf16[3072,128]{1,0:T(8,128)(2,1)S(1)}, bf16[3072,128]{1,0:T(8,128)(2,1)S(1)}, u32[]{:S(2)}, u32[]{:S(2)}) collective-permute-start(bf16[3072,128]{1,0:T(8,128)(2,1)S(1)} %collective-permute-done.1), channel_id=1, source_target_pairs={{0,64},{64,128},{128,192},{192,256},{256,320},{320,384},{384,448},... | collective-permute-start | bytes 2359304 | tf_op jit(solution)/shard_map/ppermute | solution.py:15
  41.2 7.7 %collective-permute-done.2 = bf16[3072,128]{1,0:T(8,128)(2,1)S(1)} collective-permute-done((bf16[3072,128]{1,0:T(8,128)(2,1)S(1)}, bf16[3072,128]{1,0:T(8,128)(2,1)S(1)}, u32[]{:S(2)}, u32[]{:S(2)}) %collective-permute-start.2) | collective-permute-done | bytes 786464 | tf_op jit(solution)/shard_map/ppermute | solution.py:15
  48.9 8.2 %collective-permute-start.3 = (bf16[3072,128]{1,0:T(8,128)(2,1)S(1)}, bf16[3072,128]{1,0:T(8,128)(2,1)S(1)}, u32[]{:S(2)}, u32[]{:S(2)}) collective-permute-start(bf16[3072,128]{1,0:T(8,128)(2,1)S(1)} %collective-permute-done.2), channel_id=1, source_target_pairs={{0,64},{64,128},{128,192},{192,256},{256,320},{320,384},{384,448},... | collective-permute-start | bytes 2359304 | tf_op jit(solution)/shard_map/ppermute | solution.py:15
  58.5 2.3 reduce-window.6
  62.3 11.4 %collective-permute-start.4 = (bf16[3072,128]{1,0:T(8,128)(2,1)S(1)}, bf16[3072,128]{1,0:T(8,128)(2,1)S(1)}, u32[]{:S(2)}, u32[]{:S(2)}) collective-permute-start(bf16[3072,128]{1,0:T(8,128)(2,1)S(1)} %collective-permute-done.3), channel_id=1, source_target_pairs={{0,64},{64,128},{128,192},{192,256},{256,320},{320,384},{384,448},... | collective-permute-start | bytes 2359304 | tf_op jit(solution)/shard_map/ppermute | solution.py:15
  74.1 4.3 scatter_custom_fusion.8
  78.6 2.7 collective-permute-done.4
  81.2 11.2 %collective-permute-start.5 = (bf16[3072,128]{1,0:T(8,128)(2,1)S(1)}, bf16[3072,128]{1,0:T(8,128)(2,1)}, u32[]{:S(2)}, u32[]{:S(2)}) collective-permute-start(bf16[3072,128]{1,0:T(8,128)(2,1)S(1)} %collective-permute-done.4), channel_id=1, source_target_pairs={{0,64},{64,128},{128,192},{192,256},{256,320},{320,384},{384,448},... | collective-permute-start | bytes 2359304 | tf_op jit(solution)/shard_map/ppermute | solution.py:15
  92.6 3.7 collective-permute-done.5
  96.3 11.8 %collective-permute-start.6 = (bf16[3072,128]{1,0:T(8,128)(2,1)}, bf16[3072,128]{1,0:T(8,128)(2,1)}, u32[]{:S(2)}, u32[]{:S(2)}) collective-permute-start(bf16[3072,128]{1,0:T(8,128)(2,1)} %collective-permute-done.5), channel_id=1, source_target_pairs={{0,64},{64,128},{128,192},{192,256},{256,320},{320,384},{384,448},... | collective-permute-start | bytes 2359304 | tf_op jit(solution)/shard_map/ppermute | solution.py:15
  108.1 49.3 %all-gather.2.cloned.1.call-done = bf16[512,3072]{1,0:T(8,128)(2,1)} async-done(((bf16[8,3072]{1,0:T(8,128)(2,1)}), bf16[512,3072]{1,0:T(8,128)(2,1)}) %all-gather.2.cloned.1.call-update) | async-done | bytes 3145744 | tf_op jit(solution)/shard_map/all_gather | solution.py:31
  157.3 2.1 concatenate.10
  159.5 2.7 gather_fusion
  162.2 2.2 fusion.33
  164.3 2.8 gather_fusion.1
  167.1 2.7 gather_fusion.2
  169.8 2.7 gather_fusion.3
  172.6 2.7 gather_fusion.4
  175.3 2.7 gather_fusion.5
  178.0 2.7 gather_fusion.6
  180.7 2.7 gather_fusion.7
  184.7 2.3 fusion.35
  190.5 1.8 fusion.37
  195.7 1.7 fusion.39
  198.8 1.7 fusion.40
  201.9 1.7 fusion.41
  207.0 2.9 convolution_convert_fusion
  209.9 1.9 collective-permute-start.7
  212.7 11.0 %collective-permute-done.7 = bf16[3072,128]{1,0:T(8,128)(2,1)} collective-permute-done((bf16[3072,128]{1,0:T(8,128)(2,1)}, bf16[3072,128]{1,0:T(8,128)(2,1)}, u32[]{:S(2)}, u32[]{:S(2)}) %collective-permute-start.7) | collective-permute-done | bytes 786464 | tf_op jit(solution)/shard_map/ppermute | solution.py:15
  223.7 3.1 add_convert_fusion.6
  226.8 1.9 collective-permute-start.8
  230.2 10.2 %collective-permute-done.8 = bf16[3072,128]{1,0:T(8,128)(2,1)} collective-permute-done((bf16[3072,128]{1,0:T(8,128)(2,1)}, bf16[3072,128]{1,0:T(8,128)(2,1)}, u32[]{:S(2)}, u32[]{:S(2)}) %collective-permute-start.8) | collective-permute-done | bytes 786464 | tf_op jit(solution)/shard_map/ppermute | solution.py:15
  240.4 2.2 add_convert_fusion.5
  242.6 1.9 collective-permute-start.9
  246.0 10.2 %collective-permute-done.9 = bf16[3072,128]{1,0:T(8,128)(2,1)} collective-permute-done((bf16[3072,128]{1,0:T(8,128)(2,1)}, bf16[3072,128]{1,0:T(8,128)(2,1)}, u32[]{:S(2)}, u32[]{:S(2)}) %collective-permute-start.9) | collective-permute-done | bytes 786464 | tf_op jit(solution)/shard_map/ppermute | solution.py:15
  256.2 2.2 add_convert_fusion.4
  258.4 2.1 collective-permute-start.10
  262.1 10.0 %collective-permute-done.10 = bf16[3072,128]{1,0:T(8,128)(2,1)} collective-permute-done((bf16[3072,128]{1,0:T(8,128)(2,1)}, bf16[3072,128]{1,0:T(8,128)(2,1)}, u32[]{:S(2)}, u32[]{:S(2)}) %collective-permute-start.10) | collective-permute-done | bytes 786464 | tf_op jit(solution)/shard_map/ppermute | solution.py:15
  272.0 2.2 add_convert_fusion.3
  274.3 3.3 collective-permute-start.11
  279.1 8.7 %collective-permute-done.11 = bf16[3072,128]{1,0:T(8,128)(2,1)} collective-permute-done((bf16[3072,128]{1,0:T(8,128)(2,1)}, bf16[3072,128]{1,0:T(8,128)(2,1)}, u32[]{:S(2)}, u32[]{:S(2)}) %collective-permute-start.11) | collective-permute-done | bytes 786464 | tf_op jit(solution)/shard_map/ppermute | solution.py:15
  287.9 2.2 add_convert_fusion.2
  290.1 5.1 %collective-permute-start.12 = (bf16[3072,128]{1,0:T(8,128)(2,1)}, bf16[3072,128]{1,0:T(8,128)(2,1)}, u32[]{:S(2)}, u32[]{:S(2)}) collective-permute-start(bf16[3072,128]{1,0:T(8,128)(2,1)} %add_convert_fusion.2), channel_id=1, source_target_pairs={{0,64},{64,128},{128,192},{192,256},{256,320},{320,384},{384,448},... | collective-permute-start | bytes 2359304 | tf_op jit(solution)/shard_map/ppermute | solution.py:15
  295.2 12.6 %copy.38 = bf16[1,3072,128]{2,0,1:T(2,128)(2,1)S(1)} copy(bf16[1,3072,128]{2,1,0:T(8,128)(2,1)S(1)} %copy-done.11) | data formatting | bytes 1572864 | tf_op args[4]
  308.3 17.7 %reduce.7 = bf16[3072,128]{1,0:T(8,128)(2,1)} reduce(bf16[3072,1,128]{2,1,0:T(2,128)(2,1)S(1)} %bitcast.153, bf16[]{:T(256)} %broadcast.852), dimensions={1}, to_apply=%bitcast.151.reduce_sub_computation | reduce | bytes 1572866
  326.1 2.9 reshape.1160
  328.9 11.9 %all-to-all-start = ((bf16[64,2,3072]{2,1,0:T(2,128)(2,1)}), bf16[64,2,3072]{2,1,0:T(2,128)(2,1)}, u32[]{:S(2)}, u32[]{:S(2)}) async-start(bf16[64,2,3072]{2,1,0:T(2,128)(2,1)} %reshape.1160), calls=%async_computation | async-start | bytes 1572864 | tf_op jit(solution)/shard_map/all_to_all | solution.py:75
  343.7 5.9 %collective-permute-start.13 = (bf16[3072,128]{1,0:T(8,128)(2,1)S(1)}, bf16[3072,128]{1,0:T(8,128)(2,1)S(1)}, u32[]{:S(2)}, u32[]{:S(2)}) collective-permute-start(bf16[3072,128]{1,0:T(8,128)(2,1)S(1)} %add_convert_fusion.1), channel_id=1, source_target_pairs={{0,64},{64,128},{128,192},{192,256},{256,320},{320,384},{384,448},... | collective-permute-start | bytes 2359304 | tf_op jit(solution)/shard_map/ppermute | solution.py:15
  351.1 33.3 %collective-permute-done.13 = bf16[3072,128]{1,0:T(8,128)(2,1)S(1)} collective-permute-done((bf16[3072,128]{1,0:T(8,128)(2,1)S(1)}, bf16[3072,128]{1,0:T(8,128)(2,1)S(1)}, u32[]{:S(2)}, u32[]{:S(2)}) %collective-permute-start.13) | collective-permute-done | bytes 786464 | tf_op jit(solution)/shard_map/ppermute | solution.py:15
  384.6 2.2 collective-permute-start.14
  386.8 11.1 %collective-permute-done.14 = bf16[3072,128]{1,0:T(8,128)(2,1)S(1)} collective-permute-done((bf16[3072,128]{1,0:T(8,128)(2,1)S(1)}, bf16[3072,128]{1,0:T(8,128)(2,1)S(1)}, u32[]{:S(2)}, u32[]{:S(2)}) %collective-permute-start.14) | collective-permute-done | bytes 786464 | tf_op jit(solution)/shard_map/ppermute | solution.py:15
  397.9 12.5 %copy.37 = bf16[1,3072,128]{2,0,1:T(2,128)(2,1)S(1)} copy(bf16[1,3072,128]{2,1,0:T(8,128)(2,1)S(1)} %bitcast.159) | data formatting | bytes 1572864 | tf_op jit(solution)/shard_map/broadcast_in_dim | solution.py:74
  410.4 16.9 %reduce.6 = bf16[3072,128]{1,0:T(8,128)(2,1)S(1)} reduce(bf16[3072,1,128]{2,1,0:T(2,128)(2,1)S(1)} %bitcast.154, bf16[]{:T(256)} %broadcast.852), dimensions={1}, to_apply=%bitcast.150.reduce_sub_computation | reduce | bytes 1572866
  428.3 17.6 %all-to-all-start.1 = ((bf16[64,2,3072]{2,1,0:T(2,128)(2,1)}), bf16[64,2,3072]{2,1,0:T(2,128)(2,1)}, u32[]{:S(2)}, u32[]{:S(2)}) async-start(bf16[64,2,3072]{2,1,0:T(2,128)(2,1)} %reshape.1158), calls=%async_computation.1 | async-start | bytes 1572864 | tf_op jit(solution)/shard_map/all_to_all | solution.py:74
  445.9 4.9 reshape.1161
  450.9 2.2 convert_multiply_fusion.4
  453.1 37.5 %all-to-all-done.1 = bf16[64,2,3072]{2,1,0:T(2,128)(2,1)} async-done(((bf16[64,2,3072]{2,1,0:T(2,128)(2,1)}), bf16[64,2,3072]{2,1,0:T(2,128)(2,1)}, u32[]{:S(2)}, u32[]{:S(2)}) %all-to-all-start.1) | async-done | bytes 786464 | tf_op jit(solution)/shard_map/all_to_all | solution.py:74
  490.6 4.9 reshape.1159
  495.5 3.3 convert_multiply_fusion.2
  498.8 2.0 fusion.6
  (116 shorter events, 31.0 us)
Async XLA Ops:
  7.2 66.7 %copy-start.23 = (s32[2]{0:T(128)S(1)}, s32[2]{0:T(128)}, u32[]{:S(2)}) copy-start(s32[2]{0:T(128)} %constant.170) | copy-start | bytes 28
  7.2 66.8 %copy-start.22 = (s32[2]{0:T(128)S(1)}, s32[2]{0:T(128)}, u32[]{:S(2)}) copy-start(s32[2]{0:T(128)} %constant.173) | copy-start | bytes 28
  7.2 150.1 %all-gather.2.cloned.1.call-start = ((), (), s32[]{:S(2)}) async-start(), calls=%async_computation.2 | async-start | bytes 3194880 | tf_op jit(solution)/shard_map/all_gather | solution.py:31
  7.9 13.5 %collective-permute-start = (bf16[3072,128]{1,0:T(8,128)(2,1)}, bf16[3072,128]{1,0:T(8,128)(2,1)S(1)}, u32[]{:S(2)}, u32[]{:S(2)}) collective-permute-start(bf16[3072,128]{1,0:T(8,128)(2,1)} %bitcast.158), channel_id=1, source_target_pairs={{0,64},{64,128},{128,192},{192,256},{256,320},{320,384},{384,448},... | collective-permute-start | bytes 2359304 | tf_op jit(solution)/shard_map/ppermute | solution.py:15
  21.4 27.5 %copy-start.12 = (bf16[3072,128]{1,0:T(8,128)(2,1)}, bf16[3072,128]{1,0:T(8,128)(2,1)S(1)}, u32[]{:S(2)}) copy-start(bf16[3072,128]{1,0:T(8,128)(2,1)S(1)} %collective-permute-done) | copy-start | bytes 2359300
  21.4 13.3 %collective-permute-start.1 = (bf16[3072,128]{1,0:T(8,128)(2,1)S(1)}, bf16[3072,128]{1,0:T(8,128)(2,1)S(1)}, u32[]{:S(2)}, u32[]{:S(2)}) collective-permute-start(bf16[3072,128]{1,0:T(8,128)(2,1)S(1)} %collective-permute-done), channel_id=1, source_target_pairs={{0,64},{64,128},{128,192},{192,256},{256,320},{320,384},{384,448},... | collective-permute-start | bytes 2359304 | tf_op jit(solution)/shard_map/ppermute | solution.py:15
  34.7 14.2 %copy-start.13 = (bf16[3072,128]{1,0:T(8,128)(2,1)}, bf16[3072,128]{1,0:T(8,128)(2,1)S(1)}, u32[]{:S(2)}) copy-start(bf16[3072,128]{1,0:T(8,128)(2,1)S(1)} %collective-permute-done.1) | copy-start | bytes 2359300
  34.7 14.2 %collective-permute-start.2 = (bf16[3072,128]{1,0:T(8,128)(2,1)S(1)}, bf16[3072,128]{1,0:T(8,128)(2,1)S(1)}, u32[]{:S(2)}, u32[]{:S(2)}) collective-permute-start(bf16[3072,128]{1,0:T(8,128)(2,1)S(1)} %collective-permute-done.1), channel_id=1, source_target_pairs={{0,64},{64,128},{128,192},{192,256},{256,320},{320,384},{384,448},... | collective-permute-start | bytes 2359304 | tf_op jit(solution)/shard_map/ppermute | solution.py:15
  48.9 59.1 %copy-start.15 = (bf16[3072,128]{1,0:T(8,128)(2,1)}, bf16[3072,128]{1,0:T(8,128)(2,1)S(1)}, u32[]{:S(2)}) copy-start(bf16[3072,128]{1,0:T(8,128)(2,1)S(1)} %collective-permute-done.2) | copy-start | bytes 2359300
  48.9 13.4 %collective-permute-start.3 = (bf16[3072,128]{1,0:T(8,128)(2,1)S(1)}, bf16[3072,128]{1,0:T(8,128)(2,1)S(1)}, u32[]{:S(2)}, u32[]{:S(2)}) collective-permute-start(bf16[3072,128]{1,0:T(8,128)(2,1)S(1)} %collective-permute-done.2), channel_id=1, source_target_pairs={{0,64},{64,128},{128,192},{192,256},{256,320},{320,384},{384,448},... | collective-permute-start | bytes 2359304 | tf_op jit(solution)/shard_map/ppermute | solution.py:15
  62.3 45.7 %copy-start.16 = (bf16[3072,128]{1,0:T(8,128)(2,1)}, bf16[3072,128]{1,0:T(8,128)(2,1)S(1)}, u32[]{:S(2)}) copy-start(bf16[3072,128]{1,0:T(8,128)(2,1)S(1)} %collective-permute-done.3) | copy-start | bytes 2359300
  62.3 18.9 %collective-permute-start.4 = (bf16[3072,128]{1,0:T(8,128)(2,1)S(1)}, bf16[3072,128]{1,0:T(8,128)(2,1)S(1)}, u32[]{:S(2)}, u32[]{:S(2)}) collective-permute-start(bf16[3072,128]{1,0:T(8,128)(2,1)S(1)} %collective-permute-done.3), channel_id=1, source_target_pairs={{0,64},{64,128},{128,192},{192,256},{256,320},{320,384},{384,448},... | collective-permute-start | bytes 2359304 | tf_op jit(solution)/shard_map/ppermute | solution.py:15
  81.2 26.8 %copy-start.18 = (bf16[3072,128]{1,0:T(8,128)(2,1)}, bf16[3072,128]{1,0:T(8,128)(2,1)S(1)}, u32[]{:S(2)}) copy-start(bf16[3072,128]{1,0:T(8,128)(2,1)S(1)} %collective-permute-done.4) | copy-start | bytes 2359300
  81.2 15.0 %collective-permute-start.5 = (bf16[3072,128]{1,0:T(8,128)(2,1)S(1)}, bf16[3072,128]{1,0:T(8,128)(2,1)}, u32[]{:S(2)}, u32[]{:S(2)}) collective-permute-start(bf16[3072,128]{1,0:T(8,128)(2,1)S(1)} %collective-permute-done.4), channel_id=1, source_target_pairs={{0,64},{64,128},{128,192},{192,256},{256,320},{320,384},{384,448},... | collective-permute-start | bytes 2359304 | tf_op jit(solution)/shard_map/ppermute | solution.py:15
  96.3 105.6 %collective-permute-start.6 = (bf16[3072,128]{1,0:T(8,128)(2,1)}, bf16[3072,128]{1,0:T(8,128)(2,1)}, u32[]{:S(2)}, u32[]{:S(2)}) collective-permute-start(bf16[3072,128]{1,0:T(8,128)(2,1)} %collective-permute-done.5), channel_id=1, source_target_pairs={{0,64},{64,128},{128,192},{192,256},{256,320},{320,384},{384,448},... | collective-permute-start | bytes 2359304 | tf_op jit(solution)/shard_map/ppermute | solution.py:15
  184.7 3.6 copy-start.14
  186.9 1.4 copy-start.9
  188.9 1.5 copy-start.7
  190.5 3.1 copy-start.17
  192.2 1.4 copy-start.5
  194.2 1.4 copy-start.3
  197.4 1.4 copy-start.1
  200.5 1.4 copy-start
  203.6 1.3 copy-start.20
  203.6 1.3 copy-start.21
  209.9 13.8 %collective-permute-start.7 = (bf16[3072,128]{1,0:T(8,128)(2,1)}, bf16[3072,128]{1,0:T(8,128)(2,1)}, u32[]{:S(2)}, u32[]{:S(2)}) collective-permute-start(bf16[3072,128]{1,0:T(8,128)(2,1)} %convolution_convert_fusion), channel_id=1, source_target_pairs={{0,64},{64,128},{128,192},{192,256},{256,320},{320,384},{384,448},... | collective-permute-start | bytes 2359304 | tf_op jit(solution)/shard_map/ppermute | solution.py:15
  212.7 16.9 %copy-start.10 = (bf16[256,3072]{1,0:T(8,128)(2,1)S(1)}, bf16[256,3072]{1,0:T(8,128)(2,1)}, u32[]{:S(2)}) copy-start(bf16[256,3072]{1,0:T(8,128)(2,1)} %gather_fusion.2) | copy-start | bytes 4718596
  226.8 13.6 %collective-permute-start.8 = (bf16[3072,128]{1,0:T(8,128)(2,1)}, bf16[3072,128]{1,0:T(8,128)(2,1)}, u32[]{:S(2)}, u32[]{:S(2)}) collective-permute-start(bf16[3072,128]{1,0:T(8,128)(2,1)} %add_convert_fusion.6), channel_id=1, source_target_pairs={{0,64},{64,128},{128,192},{192,256},{256,320},{320,384},{384,448},... | collective-permute-start | bytes 2359304 | tf_op jit(solution)/shard_map/ppermute | solution.py:15
  230.2 15.2 %copy-start.8 = (bf16[256,3072]{1,0:T(8,128)(2,1)S(1)}, bf16[256,3072]{1,0:T(8,128)(2,1)}, u32[]{:S(2)}) copy-start(bf16[256,3072]{1,0:T(8,128)(2,1)} %gather_fusion.3) | copy-start | bytes 4718596
  242.6 13.6 %collective-permute-start.9 = (bf16[3072,128]{1,0:T(8,128)(2,1)}, bf16[3072,128]{1,0:T(8,128)(2,1)}, u32[]{:S(2)}, u32[]{:S(2)}) collective-permute-start(bf16[3072,128]{1,0:T(8,128)(2,1)} %add_convert_fusion.5), channel_id=1, source_target_pairs={{0,64},{64,128},{128,192},{192,256},{256,320},{320,384},{384,448},... | collective-permute-start | bytes 2359304 | tf_op jit(solution)/shard_map/ppermute | solution.py:15
  246.0 15.4 %copy-start.6 = (bf16[256,3072]{1,0:T(8,128)(2,1)S(1)}, bf16[256,3072]{1,0:T(8,128)(2,1)}, u32[]{:S(2)}) copy-start(bf16[256,3072]{1,0:T(8,128)(2,1)} %gather_fusion.4) | copy-start | bytes 4718596
  258.4 13.6 %collective-permute-start.10 = (bf16[3072,128]{1,0:T(8,128)(2,1)}, bf16[3072,128]{1,0:T(8,128)(2,1)}, u32[]{:S(2)}, u32[]{:S(2)}) collective-permute-start(bf16[3072,128]{1,0:T(8,128)(2,1)} %add_convert_fusion.4), channel_id=1, source_target_pairs={{0,64},{64,128},{128,192},{192,256},{256,320},{320,384},{384,448},... | collective-permute-start | bytes 2359304 | tf_op jit(solution)/shard_map/ppermute | solution.py:15
  262.1 16.4 %copy-start.4 = (bf16[256,3072]{1,0:T(8,128)(2,1)S(1)}, bf16[256,3072]{1,0:T(8,128)(2,1)}, u32[]{:S(2)}) copy-start(bf16[256,3072]{1,0:T(8,128)(2,1)} %gather_fusion.5) | copy-start | bytes 4718596
  274.3 13.6 %collective-permute-start.11 = (bf16[3072,128]{1,0:T(8,128)(2,1)}, bf16[3072,128]{1,0:T(8,128)(2,1)}, u32[]{:S(2)}, u32[]{:S(2)}) collective-permute-start(bf16[3072,128]{1,0:T(8,128)(2,1)} %add_convert_fusion.3), channel_id=1, source_target_pairs={{0,64},{64,128},{128,192},{192,256},{256,320},{320,384},{384,448},... | collective-permute-start | bytes 2359304 | tf_op jit(solution)/shard_map/ppermute | solution.py:15
  279.1 16.1 %copy-start.11 = (bf16[1,3072,128]{2,1,0:T(8,128)(2,1)S(1)}, bf16[1,3072,128]{2,1,0:T(8,128)(2,1)}, u32[]{:S(2)}) copy-start(bf16[1,3072,128]{2,1,0:T(8,128)(2,1)} %param.10) | copy-start | bytes 2359300
  290.1 52.3 %collective-permute-start.12 = (bf16[3072,128]{1,0:T(8,128)(2,1)}, bf16[3072,128]{1,0:T(8,128)(2,1)}, u32[]{:S(2)}, u32[]{:S(2)}) collective-permute-start(bf16[3072,128]{1,0:T(8,128)(2,1)} %add_convert_fusion.2), channel_id=1, source_target_pairs={{0,64},{64,128},{128,192},{192,256},{256,320},{320,384},{384,448},... | collective-permute-start | bytes 2359304 | tf_op jit(solution)/shard_map/ppermute | solution.py:15
  326.1 15.7 %copy-start.2 = (bf16[256,3072]{1,0:T(8,128)(2,1)S(1)}, bf16[256,3072]{1,0:T(8,128)(2,1)}, u32[]{:S(2)}) copy-start(bf16[256,3072]{1,0:T(8,128)(2,1)} %gather_fusion.6) | copy-start | bytes 4718596
  328.9 99.4 %all-to-all-start = ((bf16[64,2,3072]{2,1,0:T(2,128)(2,1)}), bf16[64,2,3072]{2,1,0:T(2,128)(2,1)}, u32[]{:S(2)}, u32[]{:S(2)}) async-start(bf16[64,2,3072]{2,1,0:T(2,128)(2,1)} %reshape.1160), calls=%async_computation | async-start | bytes 1572864 | tf_op jit(solution)/shard_map/all_to_all | solution.py:75
  343.7 40.7 %collective-permute-start.13 = (bf16[3072,128]{1,0:T(8,128)(2,1)S(1)}, bf16[3072,128]{1,0:T(8,128)(2,1)S(1)}, u32[]{:S(2)}, u32[]{:S(2)}) collective-permute-start(bf16[3072,128]{1,0:T(8,128)(2,1)S(1)} %add_convert_fusion.1), channel_id=1, source_target_pairs={{0,64},{64,128},{128,192},{192,256},{256,320},{320,384},{384,448},... | collective-permute-start | bytes 2359304 | tf_op jit(solution)/shard_map/ppermute | solution.py:15
  384.6 13.3 %collective-permute-start.14 = (bf16[3072,128]{1,0:T(8,128)(2,1)S(1)}, bf16[3072,128]{1,0:T(8,128)(2,1)S(1)}, u32[]{:S(2)}, u32[]{:S(2)}) collective-permute-start(bf16[3072,128]{1,0:T(8,128)(2,1)S(1)} %add_convert_fusion), channel_id=1, source_target_pairs={{0,64},{64,128},{128,192},{192,256},{256,320},{320,384},{384,448},... | collective-permute-start | bytes 2359304 | tf_op jit(solution)/shard_map/ppermute | solution.py:15
  428.3 62.2 %all-to-all-start.1 = ((bf16[64,2,3072]{2,1,0:T(2,128)(2,1)}), bf16[64,2,3072]{2,1,0:T(2,128)(2,1)}, u32[]{:S(2)}, u32[]{:S(2)}) async-start(bf16[64,2,3072]{2,1,0:T(2,128)(2,1)} %reshape.1158), calls=%async_computation.1 | async-start | bytes 1572864 | tf_op jit(solution)/shard_map/all_to_all | solution.py:74
  495.5 3.3 copy-start.19
Sparse Core Ops, SparseCore 0:
  12.1 145.1 all-gather.1
where the time goes:
time: 513 us; the launch traced here: 508 us
  waiting for transfers between devices  218 us (42%)
  starting transfers between devices  109 us (21%)
  local copies, waits for them, and re-layouts  87.1 us (17%)
  other arithmetic  56.4 us (11%)
  matrix products  22.3 us (4%)
  between operations  15.5 us (3%)
    ppermute x15, waiting for transfers between devices, shifted(): lax.ppermute(array, axis, [(i, (i + by) % size) for i in range(size)])  130 us
    ppermute x15, starting transfers between devices, shifted(): lax.ppermute(array, axis, [(i, (i + by) % size) for i in range(size)])  79.6 us
    all_gather x1, waiting for transfers between devices, body(): grads_all = lax.all_gather(out_grad, 'dp', axis=0, tiled=True)  49.3 us
    all_to_all x1, waiting for transfers between devices, body(): lax.all_to_all(carried[None], 'dp', split_axis=1, concat_axis=2, tiled=True)  37.5 us
    unnamed x6, other arithmetic  34.9 us
    unnamed x56, local copies, waits for them, and re-layouts  32.4 us
    gather x8, local copies, waits for them, and re-layouts, body(): upstream = grads_pad[slots // topk]  21.8 us
    all_to_all x1, starting transfers between devices, body(): lax.all_to_all(carried[None], 'dp', split_axis=1, concat_axis=2, tiled=True)  17.6 us
  transfers between devices with their start and end apart: 18, of which 15 were waited for; matrix products, arithmetic and copies ran while one was open for 27% of the time, Pallas kernels for 0%

commit v1 on v0

v1 whole, which is shorter than its diff:
```python
import functools

import jax
import jax.numpy as jnp
from jax import lax
from jax.experimental import pallas as pl
from jax.experimental.pallas import tpu as pltpu
from jax.sharding import PartitionSpec as P

beta_first = 0.9
beta_second = 0.99
step_rate = 0.01
decay_rate = 1.0
sign_width = 10.0

NZ, NX, NY, NLO, NHI = 16, 4, 4, 4, 4
CELLS = NX * NY
OWN = 7
RANGES = ((6, 4), (3, 3), (10, 3), (0, 3), (13, 3))
BF16, F32 = jnp.bfloat16, jnp.float32


def kernel(
    og_ref, w_ref, mt_ref, wr_ref, gr_ref, dr_ref,
    xb, x2, wp, ht, htq, ds, gf, gx, gy, gst,
    zs, zr, ags, agr, ws, wr, hs, hr, dsend, drecv, xs, xr, gs, grs, was, war,
):
    half = og_ref.shape[1]
    cols = w_ref.shape[1]
    expert, dp = lax.axis_index("expert"), lax.axis_index("dp")
    core, z_lo = expert % 2, expert // 2
    z_hi, x, y = dp // CELLS, (dp // NY) % NX, dp % NY
    cell = dp % CELLS
    z = z_hi * NLO + z_lo

    def at_z(zz):
        return {"expert": (zz % NLO) * 2 + core, "dp": (zz // NLO) * CELLS + cell}

    def at_cell(xx, yy):
        return {"expert": expert, "dp": z_hi * CELLS + xx * NY + yy}

    z_up, z_down = at_z((z + 1) % NZ), at_z((z + NZ - 1) % NZ)
    other = {"expert": z_lo * 2 + 1 - core, "dp": dp}

    def at_lo(lo):
        return {"expert": lo * 2 + core, "dp": dp}

    def at_dp(peer):
        return {"expert": expert, "dp": peer}

    def remote(src, dst, send, recv, device):
        return pltpu.make_async_remote_copy(
            src_ref=src, dst_ref=dst, send_sem=send, recv_sem=recv,
            device_id=device, device_id_type=pl.DeviceIdType.MESH,
        )

    barrier = pltpu.get_barrier_semaphore()

    def greet(device):
        pl.semaphore_signal(
            barrier, inc=1, device_id=device, device_id_type=pl.DeviceIdType.MESH
        )

    greet(z_up)
    greet(z_down)
    greet(other)
    for i in range(1, NLO):
        greet(at_lo((z_lo + i) % NLO))

    def greet_dp(i, carry):
        greet(at_dp((dp + i) % (NHI * CELLS)))
        return carry

    lax.fori_loop(1, NHI * CELLS, greet_dp, 0)

    xb[OWN, x, y] = og_ref[...]
    wp[:, pl.ds(pl.multiple_of(core * cols, cols), cols)] = w_ref[...]
    pl.semaphore_wait(barrier, 2 + 1 + NLO - 1 + NHI * CELLS - 1)

    def z_copy(q, step):
        device = z_down if step > 0 else z_up
        return remote(xb.at[q, x, y], xb.at[q + step, x, y], zs.at[q + step], zr.at[q + step], device)

    z_copies = []

    def z_start(q, step):
        copy = z_copy(q, step)
        copy.start()
        z_copies.append(copy)

    def z_step(k):
        z_copy(OWN + k - 1, 1).wait_recv()
        if OWN + k < NZ - 1:
            z_start(OWN + k, 1)
        if OWN - k >= 0:
            z_copy(OWN - k + 1, -1).wait_recv()
            if OWN - k > 0:
                z_start(OWN - k, -1)

    z_start(OWN, 1)
    z_start(OWN, -1)
    weight_copy = remote(
        w_ref, wp.at[:, pl.ds(pl.multiple_of(core * cols, cols), cols)], was.at[0], war.at[0], other
    )
    weight_copy.start()

    part = half // 2
    piece = part // 2

    def place(r, path, phase, source, first, width):
        slots = pl.ds(RANGES[r][0], RANGES[r][1])
        lanes = pl.ds(path * part + first, width)
        if phase == 0:
            return xb.at[slots, source, y, :, lanes] if path == 0 else xb.at[slots, x, source, :, lanes]
        return xb.at[slots, :, source, :, lanes] if path == 0 else xb.at[slots, source, :, :, lanes]

    def cell_copy(r, path, phase, kind):
        along_x = path == phase
        size = NX if along_x else NY
        mine = x if along_x else y
        right, left = (mine + 1) % size, (mine + size - 1) % size
        to = right if kind in (0, 2) else left
        device = at_cell(to, y) if along_x else at_cell(x, to)
        source = (mine, mine, left, right)[kind]
        first, width = ((0, part), (0, part), (0, piece), (piece, piece))[kind]
        ref = place(r, path, phase, source, first, width)
        return remote(ref, ref, ags.at[r, path, phase, kind], agr.at[r, path, phase, kind], device)

    cell_copies = []

    def cell_start(r, path, phase, kind):
        copy = cell_copy(r, path, phase, kind)
        copy.start()
        cell_copies.append(copy)

    def direct(r, phase):
        for path in range(2):
            cell_start(r, path, phase, 0)
            cell_start(r, path, phase, 1)

    def forward(r, phase):
        for path in range(2):
            for kind in (0, 1):
                cell_copy(r, path, phase, kind).wait_recv()
                cell_start(r, path, phase, kind + 2)

    def arrived(r, phase):
        for path in range(2):
            for kind in (2, 3):
                cell_copy(r, path, phase, kind).wait_recv()

    def turn(r):
        arrived(r, 0)
        direct(r, 1)

    rows = wr_ref.shape[0]
    my_lanes = pl.ds(pl.multiple_of(dp * cols, cols), cols)

    def weight_to(peer):
        src = w_ref.at[pl.ds(pl.multiple_of(peer * rows, rows), rows), :]
        return remote(src, wr_ref.at[:, my_lanes], ws.at[0], wr.at[0], at_dp(peer))

    def send_weight(i, carry):
        weight_to((dp + i) % (NHI * CELLS)).start()
        return carry

    def send_weights():
        pltpu.make_async_copy(
            w_ref.at[pl.ds(pl.multiple_of(dp * rows, rows), rows), :], wr_ref.at[:, my_lanes], wr.at[0]
        ).start()
        lax.fori_loop(1, NHI * CELLS, send_weight, 0)

    tokens = mt_ref.shape[2]

    def hidden_lanes(lo):
        return ht.at[:, pl.ds(pl.multiple_of(lo * tokens, tokens), tokens)]

    def send_hidden():
        pltpu.make_async_copy(mt_ref.at[z_lo], hidden_lanes(z_lo), hr.at[0]).start()
        for i in range(1, NLO):
            lo = (z_lo + i) % NLO
            remote(mt_ref.at[lo], hidden_lanes(z_lo), hs.at[i - 1], hr.at[0], at_lo(lo)).start()

    block = CELLS * 8

    def unpack(q, carry):
        row = pl.multiple_of(q * block, block)
        for first in range(0, half, 256):
            wide = xb[q, :, :, :, first:first + 256].astype(F32).reshape(CELLS, 16, 256)
            x2[pl.ds(row, block), first:first + 256] = wide[:, 0:8].reshape(block, 256).astype(BF16)
            x2[pl.ds(row, block), half + first:half + first + 256] = (
                wide[:, 8:16].reshape(block, 256).astype(BF16)
            )
        return carry

    def backward(r):
        first, slots = RANGES[r]
        lax.fori_loop(first, first + slots, unpack, 0)
        low, high = first * block, (first + slots) * block
        ds[low:high, :] = jnp.dot(x2[low:high, :], wp[...], preferred_element_type=F32)
        for q in range(first, first + slots):
            zz = (z + q + NZ - OWN) % NZ
            src = ds.at[pl.ds(q * block, block), :]
            dst = dr_ref.at[z_lo, pl.ds(pl.multiple_of((zz // NLO) * block, block), block), :]
            if (q - OWN) % NLO == 0:
                pltpu.make_async_copy(src, dst, drecv.at[0]).start()
            else:
                remote(src, dst, dsend.at[q], drecv.at[0], at_lo(zz % NLO)).start()

    z_step(1)
    z_step(2)
    direct(0, 0)
    z_step(3)
    forward(0, 0)
    z_step(4)
    direct(1, 0)
    turn(0)
    z_step(5)
    direct(2, 0)
    forward(1, 0)
    z_step(6)
    turn(1)
    forward(2, 0)
    z_step(7)
    direct(3, 0)
    turn(2)
    z_step(8)
    direct(4, 0)
    forward(3, 0)
    turn(3)
    forward(4, 0)
    turn(4)
    send_weights()
    send_hidden()
    forward(0, 1)
    weight_copy.wait_recv()
    forward(1, 1)
    arrived(0, 1)
    backward(0)
    forward(2, 1)
    arrived(1, 1)
    backward(1)
    forward(3, 1)
    arrived(2, 1)
    backward(2)
    forward(4, 1)
    arrived(3, 1)
    backward(3)
    arrived(4, 1)
    backward(4)

    pltpu.make_async_copy(ht, ht, hr.at[0]).wait()
    for q in range(NZ):
        zz = (z + q + NZ - OWN) % NZ
        lane = pl.multiple_of((zz % NLO) * tokens + (zz // NLO) * block, block)
        htq[:, q * block:(q + 1) * block] = ht[:, pl.ds(lane, block)]

    wide_piece = CELLS * rows
    mine = pl.ds(pl.multiple_of(core * cols, cols), cols)
    theirs = pl.ds(pl.multiple_of((1 - core) * cols, cols), cols)

    def exchange(s):
        return remote(gx.at[s], gy.at[s], xs.at[s], xr.at[s], other)

    def gradient(s):
        start = ((z_hi + s) % NHI) * wide_piece

        def tile(t, carry):
            lane = pl.multiple_of(start + t * 256, 256)
            gf[s, :, pl.ds(pl.multiple_of(t * 256, 256), 256)] = jnp.dot(
                htq[...], x2[:, pl.ds(lane, 256)], preferred_element_type=F32
            )
            return carry

        lax.fori_loop(0, wide_piece // 256, tile, 0)
        gx[s] = gf[s, theirs, :].astype(BF16)
        exchange(s).start()

    def gradient_to(s, c, src):
        peer = ((z_hi + s) % NHI) * CELLS + c
        return remote(src, gr_ref.at[:, my_lanes], gs.at[0], grs.at[0], at_dp(peer))

    def deliver(s):
        exchange(s).wait_recv()
        total = gf[s, mine, :] + gy[s].astype(F32)
        gst[s * wide_piece:(s + 1) * wide_piece, :] = total.T.astype(BF16)

        def rows_of(c):
            return gst.at[pl.ds(pl.multiple_of(s * wide_piece + c * rows, rows), rows), :]

        def send(i, carry):
            c = (cell + i) % CELLS
            gradient_to(s, c, rows_of(c)).start()
            return carry

        if s == 0:
            pltpu.make_async_copy(rows_of(cell), gr_ref.at[:, my_lanes], grs.at[0]).start()
        lax.fori_loop(1 if s == 0 else 0, CELLS, send, 0)

    for s in range(NHI):
        gradient(s)
        if s > 0:
            deliver(s - 1)
    deliver(NHI - 1)

    for copy in z_copies + cell_copies:
        copy.wait_send()
    weight_copy.wait_send()
    for i in range(1, NLO):
        lo = (z_lo + i) % NLO
        remote(mt_ref.at[lo], hidden_lanes(z_lo), hs.at[i - 1], hr.at[0], at_lo(lo)).wait_send()
    for q in range(NZ):
        if (q - OWN) % NLO != 0:
            src = ds.at[pl.ds(q * block, block), :]
            remote(src, src, dsend.at[q], drecv.at[0], other).wait_send()
    for s in range(NHI):
        exchange(s).wait_send()
    sent = w_ref.at[pl.ds(0, (NHI * CELLS - 1) * rows), :]
    pltpu.make_async_copy(sent, sent, ws.at[0]).wait()
    sent = gst.at[pl.ds(0, (NHI * CELLS - 1) * rows), :]
    pltpu.make_async_copy(sent, sent, gs.at[0]).wait()
    pltpu.make_async_copy(wr_ref, wr_ref, wr.at[0]).wait()
    pltpu.make_async_copy(dr_ref, dr_ref, drecv.at[0]).wait()
    pltpu.make_async_copy(gr_ref, gr_ref, grs.at[0]).wait()


def exchange_all(og, weight, hidden):
    half = og.shape[1]
    width, cols = weight.shape
    tokens = hidden.shape[2]
    rows = width // (NHI * CELLS)
    ff = cols * NHI * CELLS
    total = NZ * CELLS * 8
    any_space = pl.BlockSpec(memory_space=pl.ANY)
    vmem = pl.BlockSpec(memory_space=pltpu.VMEM)
    dma = pltpu.SemaphoreType.DMA
    return pl.pallas_call(
        kernel,
        out_shape=(
            jax.ShapeDtypeStruct((rows, ff), BF16),
            jax.ShapeDtypeStruct((rows, ff), BF16),
            jax.ShapeDtypeStruct((NLO, tokens, 2 * cols), F32),
        ),
        in_specs=[vmem] * 3,
        out_specs=(any_space,) * 3,
        scratch_shapes=[
            pltpu.VMEM((NZ, NX, NY, 16, half), BF16),
            pltpu.VMEM((total, width), BF16),
            pltpu.VMEM((width, 2 * cols), BF16),
            pltpu.VMEM((2 * cols, total), BF16),
            pltpu.VMEM((2 * cols, total), BF16),
            pltpu.VMEM((total, 2 * cols), F32),
            pltpu.VMEM((NHI, 2 * cols, width // NHI), F32),
            pltpu.VMEM((NHI, cols, width // NHI), BF16),
            pltpu.VMEM((NHI, cols, width // NHI), BF16),
            pltpu.VMEM((width, cols), BF16),
            dma((NZ,)), dma((NZ,)),
            dma((len(RANGES), 2, 2, 4)), dma((len(RANGES), 2, 2, 4)),
            dma((1,)), dma((1,)),
            dma((NLO - 1,)), dma((1,)),
            dma((NZ,)), dma((1,)),
            dma((NHI,)), dma((NHI,)),
            dma((1,)), dma((1,)),
            dma((1,)), dma((1,)),
        ],
        compiler_params=pltpu.CompilerParams(
            collective_id=0, has_side_effects=True, vmem_limit_bytes=56 * 1024 * 1024
        ),
    )(og, weight, hidden)


def body(out_grad, gate_saved, up_saved, routing, down_weight, momentum):
    group_tok, topk, cols = gate_saved.shape
    experts = lax.axis_size("expert")
    own_tok, width = out_grad.shape
    half = width // 2
    og = out_grad.reshape(own_tok, 2, half).transpose(1, 0, 2).reshape(2 * own_tok, half)
    gate = gate_saved.astype(F32)
    up = up_saved.astype(F32)
    sigma = jax.nn.sigmoid(gate)
    hidden = (gate * sigma * up).astype(BF16).transpose(1, 2, 0)
    ids = jnp.arange(experts, dtype=jnp.int32)[:, None, None]
    named = [routing[:, k][None, None, :] == ids for k in range(topk)]
    none = jnp.zeros((), BF16)
    sent = jnp.where(named[0], hidden[0][None], jnp.where(named[1], hidden[1][None], none))
    sent = sent.reshape(experts // 2, 2 * cols, group_tok)
    shard_weight, shard_grad, back = exchange_all(og, down_weight[0], sent)

    dh = jnp.zeros((group_tok, topk, cols), F32)
    for e in range(experts):
        one = back[e // 2, :, (e % 2) * cols:(e % 2 + 1) * cols]
        dh = jnp.where(routing[:, :, None] == e, one[:, None, :], dh)
    d_up = (dh * gate * sigma).astype(BF16)
    d_gate = (dh * up * sigma * (1.0 + gate * (1.0 - sigma))).astype(BF16)

    grad = shard_grad[None].astype(F32)
    moment = momentum.astype(F32)
    mix = beta_first * moment + (1.0 - beta_first) * grad
    new_weight = shard_weight[None].astype(F32) * (
        1.0 - step_rate * decay_rate
    ) - step_rate * jnp.tanh(mix / sign_width)
    new_momentum = (beta_second * moment + (1.0 - beta_second) * grad).astype(BF16)
    return (d_gate, d_up, new_weight, new_momentum)


def solution(mesh):
    placed = (
        P(("expert", "dp"), None),
        P("expert", None, "dp"),
        P("expert", None, "dp"),
        P("expert", None),
        P("expert", None, "dp"),
        P("expert", "dp", None),
    )
    return jax.shard_map(
        body,
        mesh=mesh,
        in_specs=placed,
        out_specs=(
            P("expert", None, "dp"),
            P("expert", None, "dp"),
            P("expert", "dp", None),
            P("expert", "dp", None),
        ),
        check_vma=False,
    )
```

time: 513 us -> 222 us (0.43)
  the two profiles are of different devices: /device:TPU:96 before, /device:TPU:32 now
where the time goes in v1:
time: 222 us
  Pallas kernels  209 us (94%)
  local copies, waits for them, and re-layouts  6.69 us (3%)
  other arithmetic  5.24 us (2%)
    pallas_call x1, Pallas kernels, exchange_all(): pl.pallas_call(kernel, out_shape=(jax.ShapeDtypeStruct((rows, ff), BF16),...  209 us

profile of v1, /device:TPU:32, one launch (start us, length us, event | category | flops | bytes accessed | tf_op | source)
XLA Modules:
  0.0 221.6 jit_solution(17104668212521476889)
XLA Ops:
  0.6 0.0 copy-start.1
  0.6 1.1 copy.20
  1.8 1.1 copy.21
  2.9 0.2 fusion.19
  3.1 0.0 copy-done.1
  3.1 1.1 select_select_fusion
  4.2 208.9 %shard_map.93 = (bf16[48,8192]{1,0:T(8,128)(2,1)}, bf16[48,8192]{1,0:T(8,128)(2,1)}, f32[4,512,256]{2,1,0:T(8,128)}) custom-call(bf16[16,1536]{1,0:T(8,128)(2,1)} %bitcast.43, bf16[3072,128]{1,0:T(8,128)(2,1)} %bitcast.42, bf16[4,256,512]{2,1,0:T(8,128)(2,1)} %bitcast.41), custom_call_target="tpu_custom_call" | custom-call | tf_op jit(solution)/shard_map/pallas_call | solution.py:337
  213.1 1.7 slice_bitcast_fusion.7
  214.8 0.1 copy.22
  214.9 0.1 copy.23
  215.0 0.1 copy.24
  215.2 0.1 copy.25
  215.3 0.1 copy.26
  215.5 0.1 copy.27
  215.6 0.1 copy.28
  215.7 0.1 copy.29
  215.9 0.4 fusion.18
  216.3 0.0 copy-start
  216.3 0.9 copy.30
  217.2 0.9 copy.31
  218.1 0.0 copy-done
  218.1 3.5 %fusion.6 = (bf16[1,48,8192]{2,1,0:T(8,128)(2,1)}, f32[1,48,8192]{2,1,0:T(8,128)}) fusion(bf16[1,48,8192]{2,1,0:T(8,128)(2,1)S(1)} %copy-done, bf16[48,8192]{1,0:T(8,128)(2,1)} %get-tuple-element.9, bf16[48,8192]{1,0:T(8,128)(2,1)} %get-tuple-element.8), kind=kLoop, calls=%fused_computation.10 | loop fusion | flops 5505024 | bytes 4718592 | tf_op jit(solution)/shard_map/convert_element_type | solution.py:402
  (4 shorter events, 0.1 us)
Async XLA Ops:
  0.6 2.5 %copy-start.1 = (s32[512,2]{0,1:T(2,128)S(1)}, s32[512,2]{0,1:T(2,128)}, u32[]{:S(2)}) copy-start(s32[512,2]{0,1:T(2,128)} %param.9) | copy-start | bytes 12292
  216.3 1.8 copy-start

commit v2 on v1

v2 whole, which is shorter than its diff:
```python
import functools

import jax
import jax.numpy as jnp
from jax import lax
from jax.experimental import pallas as pl
from jax.experimental.pallas import tpu as pltpu
from jax.sharding import PartitionSpec as P

beta_first = 0.9
beta_second = 0.99
step_rate = 0.01
decay_rate = 1.0
sign_width = 10.0

NZ, NX, NY, NLO, NHI = 16, 4, 4, 4, 4
CELLS = NX * NY
PAIR = 4
SLOTS = NZ // 2
OWN = SLOTS // 2 - 1
RANGES = ((2, 4), (0, 2), (6, 2))
BF16, F32 = jnp.bfloat16, jnp.float32


def kernel(
    og_ref, w_ref, hid_ref, wr_ref, gr_ref, dr_ref,
    xb, x2, wp, ht, htq, mk, dn, ds, gf, gx, gy, gu, px, py, gst,
    zs, zr, ags, agr, ws, wr, hs, hr, dsend, drecv, xs, xr, ps, pr, gs, grs, was, war,
):
    half = og_ref.shape[1]
    cols = w_ref.shape[1]
    expert, dp = lax.axis_index("expert"), lax.axis_index("dp")
    core, z_lo = expert % 2, expert // 2
    z_hi, x, y = dp // CELLS, (dp // NY) % NX, dp % NY
    cell = dp % CELLS
    z = z_hi * NLO + z_lo
    side, pair = z_lo % 2, z_lo // 2
    beside = pair * 2 + 1 - side
    across = (z_lo + 2) % NLO

    def at_z(zz):
        return {"expert": (zz % NLO) * 2 + core, "dp": (zz // NLO) * CELLS + cell}

    def at_cell(xx, yy):
        return {"expert": expert, "dp": z_hi * CELLS + xx * NY + yy}

    def at_lo(lo):
        return {"expert": lo * 2 + core, "dp": dp}

    def at_dp(peer):
        return {"expert": expert, "dp": peer}

    z_up, z_down = at_z((z + 2) % NZ), at_z((z + NZ - 2) % NZ)
    other = {"expert": z_lo * 2 + 1 - core, "dp": dp}

    def remote(src, dst, send, recv, device):
        return pltpu.make_async_remote_copy(
            src_ref=src, dst_ref=dst, send_sem=send, recv_sem=recv,
            device_id=device, device_id_type=pl.DeviceIdType.MESH,
        )

    barrier = pltpu.get_barrier_semaphore()

    def greet(device):
        pl.semaphore_signal(
            barrier, inc=1, device_id=device, device_id_type=pl.DeviceIdType.MESH
        )

    for device in (z_up, z_down, other, at_lo(beside), at_lo(across)):
        greet(device)

    def greet_dp(i, carry):
        greet(at_dp((dp + i) % (NHI * CELLS)))
        return carry

    lax.fori_loop(1, NHI * CELLS, greet_dp, 0)

    def expert_lanes(s, c):
        return pl.ds(pl.multiple_of((s * 2 + c) * cols, cols), cols)

    xb[OWN, x, y] = og_ref[...]
    wp[:, expert_lanes(side, core)] = w_ref[...]
    ht[0] = hid_ref[...]
    pl.semaphore_wait(barrier, 5 + NHI * CELLS - 1)

    def z_copy(q, step):
        device = z_down if step > 0 else z_up
        return remote(xb.at[q, x, y], xb.at[q + step, x, y], zs.at[q + step], zr.at[q + step], device)

    sends = []

    def start(copy):
        copy.start()
        sends.append(copy)

    def z_step(k):
        z_copy(OWN + k - 1, 1).wait_recv()
        if OWN + k < SLOTS - 1:
            start(z_copy(OWN + k, 1))
        if OWN - k >= 0:
            z_copy(OWN - k + 1, -1).wait_recv()
            if OWN - k > 0:
                start(z_copy(OWN - k, -1))

    start(z_copy(OWN, 1))
    start(z_copy(OWN, -1))

    own_weight = wp.at[:, expert_lanes(side, core)]
    to_core = remote(w_ref, own_weight, was.at[0], war.at[0], other)
    to_beside = remote(w_ref, own_weight, was.at[1], war.at[1], at_lo(beside))
    from_beside = wp.at[:, expert_lanes(1 - side, core)]
    relay = remote(from_beside, from_beside, was.at[2], war.at[2], other)
    start(to_core)
    start(to_beside)

    hidden_copy = remote(hid_ref, ht.at[1], hs.at[0], hr.at[0], at_lo(across))
    start(hidden_copy)

    part = half // 2
    piece = part // 2

    def place(r, path, phase, source, first, width):
        slots = pl.ds(RANGES[r][0], RANGES[r][1])
        lanes = pl.ds(path * part + first, width)
        if phase == 0:
            return xb.at[slots, source, y, :, lanes] if path == 0 else xb.at[slots, x, source, :, lanes]
        return xb.at[slots, :, source, :, lanes] if path == 0 else xb.at[slots, source, :, :, lanes]

    def cell_copy(r, path, phase, kind):
        along_x = path == phase
        size = NX if along_x else NY
        mine = x if along_x else y
        right, left = (mine + 1) % size, (mine + size - 1) % size
        to = right if kind in (0, 2) else left
        device = at_cell(to, y) if along_x else at_cell(x, to)
        source = (mine, mine, left, right)[kind]
        first, width = ((0, part), (0, part), (0, piece), (piece, piece))[kind]
        ref = place(r, path, phase, source, first, width)
        return remote(ref, ref, ags.at[r, path, phase, kind], agr.at[r, path, phase, kind], device)

    def direct(r, phase):
        for path in range(2):
            start(cell_copy(r, path, phase, 0))
            start(cell_copy(r, path, phase, 1))

    def forward(r, phase):
        for path in range(2):
            for kind in (0, 1):
                cell_copy(r, path, phase, kind).wait_recv()
                start(cell_copy(r, path, phase, kind + 2))

    def arrived(r, phase):
        for path in range(2):
            for kind in (2, 3):
                cell_copy(r, path, phase, kind).wait_recv()

    def turn(r):
        arrived(r, 0)
        direct(r, 1)

    rows = wr_ref.shape[0]
    my_lanes = pl.ds(pl.multiple_of(dp * cols, cols), cols)

    def send_weight(i, carry):
        peer = (dp + i) % (NHI * CELLS)
        src = w_ref.at[pl.ds(pl.multiple_of(peer * rows, rows), rows), :]
        remote(src, wr_ref.at[:, my_lanes], ws.at[0], wr.at[0], at_dp(peer)).start()
        return carry

    def send_weights():
        pltpu.make_async_copy(
            w_ref.at[pl.ds(pl.multiple_of(dp * rows, rows), rows), :], wr_ref.at[:, my_lanes], wr.at[0]
        ).start()
        lax.fori_loop(1, NHI * CELLS, send_weight, 0)

    block = CELLS * 8
    tokens = dr_ref.shape[1]

    def token_lane(q):
        return pl.multiple_of(((z + 2 * (q + SLOTS - OWN)) % NZ) // NLO * block, block)

    def unpack_hidden(q):
        lane = token_lane(q)
        which = (q - OWN) % 2
        named = ht[which, 2 * cols:2 * cols + 16, pl.ds(lane, block)].astype(F32)
        first = ht[which, 0:cols, pl.ds(lane, block)].astype(F32)
        second = ht[which, cols:2 * cols, pl.ds(lane, block)].astype(F32)
        hits = []
        for e in range(PAIR):
            index = (pair * PAIR + e).astype(F32)
            one = jnp.where(named[0:1] == index, 1.0, 0.0)
            two = jnp.where(named[1:2] == index, 1.0, 0.0)
            hits.append((one, two))
            htq[e * cols:(e + 1) * cols, q * block:(q + 1) * block] = (one * first + two * second).astype(BF16)
        for k in range(2):
            for e in range(PAIR):
                mk[q, k, e] = jnp.broadcast_to(hits[e][k], (block, block)).T

    def unpack(q, carry):
        row = pl.multiple_of(q * block, block)
        for first in range(0, half, 256):
            wide = xb[q, :, :, :, first:first + 256].astype(F32).reshape(CELLS, 16, 256)
            x2[pl.ds(row, block), first:first + 256] = wide[:, 0:8].reshape(block, 256).astype(BF16)
            x2[pl.ds(row, block), half + first:half + first + 256] = (
                wide[:, 8:16].reshape(block, 256).astype(BF16)
            )
        return carry

    def dh_copy(q):
        src = ds.at[pl.ds(q * block, block), :]
        lane = token_lane(q)
        if (q - OWN) % 2 == 0:
            return pltpu.make_async_copy(src, dr_ref.at[0, pl.ds(lane, block), :], drecv.at[0])
        return remote(src, dr_ref.at[1, pl.ds(lane, block), :], dsend.at[q], drecv.at[0], at_lo(across))

    def backward(r):
        first, slots = RANGES[r]
        lax.fori_loop(first, first + slots, unpack, 0)
        low, high = first * block, (first + slots) * block
        dn[low:high, :] = jnp.dot(x2[low:high, :], wp[...], preferred_element_type=F32)
        for q in range(first, first + slots):
            unpack_hidden(q)
            at = slice(q * block, (q + 1) * block)
            for k in range(2):
                picked = mk[q, k, 0] * dn[at, 0:cols]
                for e in range(1, PAIR):
                    picked += mk[q, k, e] * dn[at, e * cols:(e + 1) * cols]
                ds[at, k * cols:(k + 1) * cols] = picked
            dh_copy(q).start()

    z_step(1)
    z_step(2)
    direct(0, 0)
    z_step(3)
    direct(1, 0)
    forward(0, 0)
    z_step(4)
    direct(2, 0)
    turn(0)
    forward(1, 0)
    forward(2, 0)
    turn(1)
    turn(2)
    send_weights()
    to_beside.wait_recv()
    start(relay)
    hidden_copy.wait_recv()
    forward(0, 1)
    forward(1, 1)
    arrived(0, 1)
    to_core.wait_recv()
    relay.wait_recv()
    backward(0)
    forward(2, 1)
    arrived(1, 1)
    backward(1)
    arrived(2, 1)
    backward(2)

    wide_piece = CELLS * rows

    def expert_rows(s, c):
        return expert_lanes(s, c)

    def over_chip(s):
        return remote(gx.at[s], gy.at[s], xs.at[s], xr.at[s], other)

    def over_pair(s):
        return remote(px.at[s], py.at[s], ps.at[s], pr.at[s], at_lo(beside))

    def gradient(s):
        begin = ((z_hi + s) % NHI) * wide_piece

        def tile(t, carry):
            lane = pl.multiple_of(begin + t * 256, 256)
            gf[s, :, pl.ds(pl.multiple_of(t * 256, 256), 256)] = jnp.dot(
                htq[...], x2[:, pl.ds(lane, 256)], preferred_element_type=F32
            )
            return carry

        lax.fori_loop(0, wide_piece // 256, tile, 0)
        gx[s, 0] = gf[s, expert_rows(side, 1 - core), :].astype(BF16)
        gx[s, 1] = gf[s, expert_rows(1 - side, 1 - core), :].astype(BF16)
        start(over_chip(s))

    def sum_chip(s):
        over_chip(s).wait_recv()
        px[s] = (gf[s, expert_rows(1 - side, core), :] + gy[s, 1].astype(F32)).astype(BF16)
        start(over_pair(s))
        gu[s] = gf[s, expert_rows(side, core), :] + gy[s, 0].astype(F32)

    def deliver(s):
        over_pair(s).wait_recv()
        total = gu[s] + py[s].astype(F32)
        gst[s * wide_piece:(s + 1) * wide_piece, :] = total.T.astype(BF16)

        def rows_of(c):
            return gst.at[pl.ds(pl.multiple_of(s * wide_piece + c * rows, rows), rows), :]

        def send(i, carry):
            c = (cell + i) % CELLS
            peer = ((z_hi + s) % NHI) * CELLS + c
            remote(rows_of(c), gr_ref.at[:, my_lanes], gs.at[0], grs.at[0], at_dp(peer)).start()
            return carry

        if s == 0:
            pltpu.make_async_copy(rows_of(cell), gr_ref.at[:, my_lanes], grs.at[0]).start()
        lax.fori_loop(1 if s == 0 else 0, CELLS, send, 0)

    for s in range(NHI + 2):
        if s < NHI:
            gradient(s)
        if 0 < s < NHI + 1:
            sum_chip(s - 1)
        if s > 1:
            deliver(s - 2)

    for copy in sends:
        copy.wait_send()
    for q in range(SLOTS):
        if (q - OWN) % 2 != 0:
            dh_copy(q).wait_send()
    sent = w_ref.at[pl.ds(0, (NHI * CELLS - 1) * rows), :]
    pltpu.make_async_copy(sent, sent, ws.at[0]).wait()
    sent = gst.at[pl.ds(0, (NHI * CELLS - 1) * rows), :]
    pltpu.make_async_copy(sent, sent, gs.at[0]).wait()
    pltpu.make_async_copy(wr_ref, wr_ref, wr.at[0]).wait()
    pltpu.make_async_copy(dr_ref, dr_ref, drecv.at[0]).wait()
    pltpu.make_async_copy(gr_ref, gr_ref, grs.at[0]).wait()


def exchange_all(og, weight, hidden):
    half = og.shape[1]
    width, cols = weight.shape
    tokens = hidden.shape[1]
    rows = width // (NHI * CELLS)
    ff = cols * NHI * CELLS
    total = SLOTS * CELLS * 8
    piece = width // NHI
    any_space = pl.BlockSpec(memory_space=pl.ANY)
    vmem = pl.BlockSpec(memory_space=pltpu.VMEM)
    dma = pltpu.SemaphoreType.DMA
    ranges = len(RANGES)
    return pl.pallas_call(
        kernel,
        out_shape=(
            jax.ShapeDtypeStruct((rows, ff), BF16),
            jax.ShapeDtypeStruct((rows, ff), BF16),
            jax.ShapeDtypeStruct((2, tokens, 2 * cols), F32),
        ),
        in_specs=[vmem] * 3,
        out_specs=(any_space,) * 3,
        scratch_shapes=[
            pltpu.VMEM((SLOTS, NX, NY, 16, half), BF16),
            pltpu.VMEM((total, width), BF16),
            pltpu.VMEM((width, PAIR * cols), BF16),
            pltpu.VMEM((2, 2 * cols + 16, tokens), BF16),
            pltpu.VMEM((PAIR * cols, total), BF16),
            pltpu.VMEM((SLOTS, 2, PAIR, CELLS * 8, cols), F32),
            pltpu.VMEM((total, PAIR * cols), F32),
            pltpu.VMEM((total, 2 * cols), F32),
            pltpu.VMEM((NHI, PAIR * cols, piece), F32),
            pltpu.VMEM((NHI, 2, cols, piece), BF16),
            pltpu.VMEM((NHI, 2, cols, piece), BF16),
            pltpu.VMEM((NHI, cols, piece), F32),
            pltpu.VMEM((NHI, cols, piece), BF16),
            pltpu.VMEM((NHI, cols, piece), BF16),
            pltpu.VMEM((width, cols), BF16),
            dma((SLOTS,)), dma((SLOTS,)),
            dma((ranges, 2, 2, 4)), dma((ranges, 2, 2, 4)),
            dma((1,)), dma((1,)),
            dma((1,)), dma((1,)),
            dma((SLOTS,)), dma((1,)),
            dma((NHI,)), dma((NHI,)),
            dma((NHI,)), dma((NHI,)),
            dma((1,)), dma((1,)),
            dma((3,)), dma((3,)),
        ],
        compiler_params=pltpu.CompilerParams(
            collective_id=0, has_side_effects=True, vmem_limit_bytes=56 * 1024 * 1024
        ),
    )(og, weight, hidden)


def body(out_grad, gate_saved, up_saved, routing, down_weight, momentum):
    group_tok, topk, cols = gate_saved.shape
    own_tok, width = out_grad.shape
    half = width // 2
    og = out_grad.reshape(own_tok, 2, half).transpose(1, 0, 2).reshape(2 * own_tok, half)
    gate = gate_saved.astype(F32)
    up = up_saved.astype(F32)
    sigma = jax.nn.sigmoid(gate)
    hidden = (gate * sigma * up).astype(BF16).transpose(1, 2, 0)
    named = jnp.zeros((16, group_tok), BF16).at[:topk].set(routing.T.astype(BF16))
    sent = jnp.concatenate([hidden.reshape(topk * cols, group_tok), named], axis=0)
    shard_weight, shard_grad, back = exchange_all(og, down_weight[0], sent)
    dh = (back[0] + back[1]).reshape(group_tok, topk, cols)
    d_up = (dh * gate * sigma).astype(BF16)
    d_gate = (dh * up * sigma * (1.0 + gate * (1.0 - sigma))).astype(BF16)

    grad = shard_grad[None].astype(F32)
    moment = momentum.astype(F32)
    mix = beta_first * moment + (1.0 - beta_first) * grad
    new_weight = shard_weight[None].astype(F32) * (
        1.0 - step_rate * decay_rate
    ) - step_rate * jnp.tanh(mix / sign_width)
    new_momentum = (beta_second * moment + (1.0 - beta_second) * grad).astype(BF16)
    return (d_gate, d_up, new_weight, new_momentum)


def solution(mesh):
    placed = (
        P(("expert", "dp"), None),
        P("expert", None, "dp"),
        P("expert", None, "dp"),
        P("expert", None),
        P("expert", None, "dp"),
        P("expert", "dp", None),
    )
    return jax.shard_map(
        body,
        mesh=mesh,
        in_specs=placed,
        out_specs=(
            P("expert", None, "dp"),
            P("expert", None, "dp"),
            P("expert", "dp", None),
            P("expert", "dp", None),
        ),
        check_vma=False,
    )
```

time: 222 us -> 183 us (0.82)
  the two profiles are of different devices: /device:TPU:32 before, /device:TPU:62 now
where the time goes in v2:
time: 183 us
  Pallas kernels  174 us (95%)
  other arithmetic  8.13 us (4%)
    pallas_call x1, Pallas kernels, exchange_all(): pl.pallas_call(kernel, out_shape=(jax.ShapeDtypeStruct((rows, ff), BF16),...  174 us

profile of v2, /device:TPU:62, one launch (start us, length us, event | category | flops | bytes accessed | tf_op | source)
XLA Modules:
  0.0 182.9 jit_solution(15255690415910903549)
XLA Ops:
  0.6 0.7 convert_bitcast_fusion
  1.3 1.7 fusion.21
  3.0 0.2 copy.10
  3.1 0.7 fusion.20.hid_ref
  3.9 173.6 %shard_map.93 = (bf16[48,8192]{1,0:T(8,128)(2,1)}, bf16[48,8192]{1,0:T(8,128)(2,1)}, f32[2,512,256]{2,1,0:T(8,128)}) custom-call(bf16[16,1536]{1,0:T(8,128)(2,1)} %bitcast.23, bf16[3072,128]{1,0:T(8,128)(2,1)} %bitcast.22, bf16[272,512]{1,0:T(8,128)(2,1)} %fusion.20.hid_ref), custom_call_target="tpu_custom_call" | custom-call | tf_op jit(solution)/shard_map/pallas_call | solution.py:344
  177.4 0.0 copy-start
  177.5 0.0 copy-start.1
  177.5 1.3 slice_add_fusion
  178.8 0.0 copy-start.2
  178.8 0.3 add.25
  179.1 0.0 copy-done
  179.1 0.0 copy-done.1
  179.1 0.0 copy-start.3
  179.1 0.0 copy-start.4
  179.1 1.6 fusion.19
  180.7 0.0 copy-done.2
  180.7 0.0 copy-done.3
  180.7 0.0 copy-done.4
  180.7 2.1 %fusion.6 = (bf16[1,48,8192]{2,1,0:T(8,128)(2,1)}, f32[1,48,8192]{2,1,0:T(8,128)}) fusion(bf16[1,48,8192]{2,1,0:T(8,128)(2,1)S(1)} %copy-done.2, bf16[48,8192]{1,0:T(8,128)(2,1)S(1)} %copy-done.4, bf16[48,8192]{1,0:T(8,128)(2,1)S(1)} %copy-done.3), kind=kLoop, calls=%fused_computation.10 | loop fusion | flops 5505024 | bytes 4718592 | tf_op jit(solution)/shard_map/convert_element_type | solution.py:407
Async XLA Ops:
  177.4 1.6 copy-start
  177.5 1.6 copy-start.1
  178.8 1.9 %copy-start.2 = (bf16[1,48,8192]{2,1,0:T(8,128)(2,1)S(1)}, bf16[1,48,8192]{2,1,0:T(8,128)(2,1)}, u32[]{:S(2)}) copy-start(bf16[1,48,8192]{2,1,0:T(8,128)(2,1)} %param.13) | copy-start | bytes 2359300
  179.1 1.6 copy-start.3
  179.1 1.6 copy-start.4

commit v3 on v2

--- a/solution.py
+++ b/solution.py
@@ -47,8 +47,12 @@
     def at_lo(lo):
         return {"expert": lo * 2 + core, "dp": dp}
 
-    def at_dp(peer):
-        return {"expert": expert, "dp": peer}
+    away = (z_hi + NHI - 1 + 2 * side) % NHI
+    toward = (z_hi + 1 + 2 * side) % NHI
+    far = (z_hi + 2) % NHI
+
+    def owner(lo, hi, c):
+        return {"expert": lo * 2 + core, "dp": hi * CELLS + c}
 
     z_up, z_down = at_z((z + 2) % NZ), at_z((z + NZ - 2) % NZ)
     other = {"expert": z_lo * 2 + 1 - core, "dp": dp}
@@ -69,11 +73,19 @@
     for device in (z_up, z_down, other, at_lo(beside), at_lo(across)):
         greet(device)
 
-    def greet_dp(i, carry):
-        greet(at_dp((dp + i) % (NHI * CELLS)))
-        return carry
-
-    lax.fori_loop(1, NHI * CELLS, greet_dp, 0)
+    def greet_cells(i, carry):
+        c = (cell + i) % CELLS
+        greet(owner(z_lo, toward, c))
+        greet(owner(beside, away, c))
+        greet(owner(beside, far, c))
+        return carry
+
+    def greet_near(i, carry):
+        greet(owner(z_lo, z_hi, (cell + i) % CELLS))
+        return carry
+
+    lax.fori_loop(0, CELLS, greet_cells, 0)
+    lax.fori_loop(1, CELLS, greet_near, 0)
 
     def expert_lanes(s, c):
         return pl.ds(pl.multiple_of((s * 2 + c) * cols, cols), cols)
@@ -111,10 +123,8 @@
     from_beside = wp.at[:, expert_lanes(1 - side, core)]
     relay = remote(from_beside, from_beside, was.at[2], war.at[2], other)
     start(to_core)
-    start(to_beside)
 
     hidden_copy = remote(hid_ref, ht.at[1], hs.at[0], hr.at[0], at_lo(across))
-    start(hidden_copy)
 
     part = half // 2
     piece = part // 2
@@ -161,17 +171,30 @@
     rows = wr_ref.shape[0]
     my_lanes = pl.ds(pl.multiple_of(dp * cols, cols), cols)
 
-    def send_weight(i, carry):
-        peer = (dp + i) % (NHI * CELLS)
-        src = w_ref.at[pl.ds(pl.multiple_of(peer * rows, rows), rows), :]
-        remote(src, wr_ref.at[:, my_lanes], ws.at[0], wr.at[0], at_dp(peer)).start()
+    def weight_rows(s, hi, c):
+        row = pl.multiple_of((hi * CELLS + c) * rows, rows)
+        return wp.at[pl.ds(row, rows), expert_lanes(s, core)]
+
+    def send_weight(lo, s, hi, c):
+        remote(weight_rows(s, hi, c), wr_ref.at[:, my_lanes], ws.at[0], wr.at[0], owner(lo, hi, c)).start()
+
+    def send_own(i, carry):
+        send_weight(z_lo, side, away, (cell + i) % CELLS)
+        return carry
+
+    def send_near(i, carry):
+        send_weight(z_lo, side, z_hi, (cell + i) % CELLS)
+        return carry
+
+    def send_beside(i, carry):
+        send_weight(beside, 1 - side, far, (cell + i) % CELLS)
+        send_weight(beside, 1 - side, away, (cell + i) % CELLS)
         return carry
 
     def send_weights():
-        pltpu.make_async_copy(
-            w_ref.at[pl.ds(pl.multiple_of(dp * rows, rows), rows), :], wr_ref.at[:, my_lanes], wr.at[0]
-        ).start()
-        lax.fori_loop(1, NHI * CELLS, send_weight, 0)
+        pltpu.make_async_copy(weight_rows(side, z_hi, cell), wr_ref.at[:, my_lanes], wr.at[0]).start()
+        lax.fori_loop(0, CELLS, send_own, 0)
+        lax.fori_loop(1, CELLS, send_near, 0)
 
     block = CELLS * 8
     tokens = dr_ref.shape[1]
@@ -226,7 +249,6 @@
                 for e in range(1, PAIR):
                     picked += mk[q, k, e] * dn[at, e * cols:(e + 1) * cols]
                 ds[at, k * cols:(k + 1) * cols] = picked
-            dh_copy(q).start()
 
     z_step(1)
     z_step(2)
@@ -236,15 +258,18 @@
     forward(0, 0)
     z_step(4)
     direct(2, 0)
+    start(to_beside)
+    start(hidden_copy)
+    send_weights()
     turn(0)
     forward(1, 0)
     forward(2, 0)
     turn(1)
     turn(2)
-    send_weights()
     to_beside.wait_recv()
     start(relay)
     hidden_copy.wait_recv()
+    lax.fori_loop(0, CELLS, send_beside, 0)
     forward(0, 1)
     forward(1, 1)
     arrived(0, 1)
@@ -258,18 +283,16 @@
     backward(2)
 
     wide_piece = CELLS * rows
-
-    def expert_rows(s, c):
-        return expert_lanes(s, c)
+    targets = (toward, far, z_hi, away)
 
     def over_chip(s):
         return remote(gx.at[s], gy.at[s], xs.at[s], xr.at[s], other)
 
-    def over_pair(s):
-        return remote(px.at[s], py.at[s], ps.at[s], pr.at[s], at_lo(beside))
+    def over_pair(slot):
+        return remote(px.at[slot], py.at[slot], ps.at[slot], pr.at[slot], at_lo(beside))
 
     def gradient(s):
-        begin = ((z_hi + s) % NHI) * wide_piece
+        begin = targets[s] * wide_piece
 
         def tile(t, carry):
             lane = pl.multiple_of(begin + t * 256, 256)
@@ -279,41 +302,64 @@
             return carry
 
         lax.fori_loop(0, wide_piece // 256, tile, 0)
-        gx[s, 0] = gf[s, expert_rows(side, 1 - core), :].astype(BF16)
-        gx[s, 1] = gf[s, expert_rows(1 - side, 1 - core), :].astype(BF16)
+        gx[s, 0] = gf[s, expert_lanes(side, 1 - core), :].astype(BF16)
+        gx[s, 1] = gf[s, expert_lanes(1 - side, 1 - core), :].astype(BF16)
         start(over_chip(s))
+
+    def chip_sum(s, own):
+        lanes = expert_lanes(side, core) if own else expert_lanes(1 - side, core)
+        return gf[s, lanes, :] + gy[s, 0 if own else 1].astype(F32)
 
     def sum_chip(s):
         over_chip(s).wait_recv()
-        px[s] = (gf[s, expert_rows(1 - side, core), :] + gy[s, 1].astype(F32)).astype(BF16)
-        start(over_pair(s))
-        gu[s] = gf[s, expert_rows(side, core), :] + gy[s, 0].astype(F32)
-
-    def deliver(s):
-        over_pair(s).wait_recv()
-        total = gu[s] + py[s].astype(F32)
-        gst[s * wide_piece:(s + 1) * wide_piece, :] = total.T.astype(BF16)
+        if s == 0:
+            px[0] = chip_sum(0, True).astype(BF16)
+            start(over_pair(0))
+            px[1] = chip_sum(0, False).astype(BF16)
+            start(over_pair(1))
+        elif s == 1:
+            px[2] = chip_sum(1, True).astype(BF16)
+            start(over_pair(2))
+            gu[0] = chip_sum(1, False)
+        elif s == 2:
+            px[3] = chip_sum(2, False).astype(BF16)
+            start(over_pair(3))
+            gu[1] = chip_sum(2, True)
+        else:
+            gu[2] = chip_sum(3, True)
+            gu[3] = chip_sum(3, False)
+
+    def deliver(part_sum, slot, lo, hi, near):
+        over_pair(slot).wait_recv()
+        total = gu[part_sum] + py[slot].astype(F32)
+        gst[part_sum * wide_piece:(part_sum + 1) * wide_piece, :] = total.T.astype(BF16)
 
         def rows_of(c):
-            return gst.at[pl.ds(pl.multiple_of(s * wide_piece + c * rows, rows), rows), :]
+            return gst.at[pl.ds(pl.multiple_of(part_sum * wide_piece + c * rows, rows), rows), :]
 
         def send(i, carry):
             c = (cell + i) % CELLS
-            peer = ((z_hi + s) % NHI) * CELLS + c
-            remote(rows_of(c), gr_ref.at[:, my_lanes], gs.at[0], grs.at[0], at_dp(peer)).start()
+            remote(rows_of(c), gr_ref.at[:, my_lanes], gs.at[0], grs.at[0], owner(lo, hi, c)).start()
             return carry
 
-        if s == 0:
+        if near:
             pltpu.make_async_copy(rows_of(cell), gr_ref.at[:, my_lanes], grs.at[0]).start()
-        lax.fori_loop(1 if s == 0 else 0, CELLS, send, 0)
-
-    for s in range(NHI + 2):
-        if s < NHI:
-            gradient(s)
-        if 0 < s < NHI + 1:
-            sum_chip(s - 1)
-        if s > 1:
-            deliver(s - 2)
+        lax.fori_loop(1 if near else 0, CELLS, send, 0)
+
+    gradient(1)
+    gradient(0)
+    sum_chip(1)
+    sum_chip(0)
+    for q in range(SLOTS):
+        dh_copy(q).start()
+    gradient(2)
+    gradient(3)
+    deliver(0, 2, beside, far, False)
+    sum_chip(2)
+    sum_chip(3)
+    deliver(3, 0, beside, away, False)
+    deliver(2, 1, z_lo, away, False)
+    deliver(1, 3, z_lo, z_hi, True)
 
     for copy in sends:
         copy.wait_send()

time: 183 us -> 163 us (0.89)
  the two profiles are of different devices: /device:TPU:62 before, /device:TPU:32 now
where the time goes in v3:
time: 163 us
  Pallas kernels  154 us (94%)
  other arithmetic  8.13 us (5%)
    pallas_call x1, Pallas kernels, exchange_all(): pl.pallas_call(kernel, out_shape=(jax.ShapeDtypeStruct((rows, ff), BF16),...  154 us

profile of v3, /device:TPU:32, one launch (start us, length us, event | category | flops | bytes accessed | tf_op | source)
XLA Modules:
  0.0 162.9 jit_solution(14449816085385736752)
XLA Ops:
  0.6 0.7 convert_bitcast_fusion
  1.3 1.7 %fusion.21 = (bf16[2,128,512]{1,0,2:T(2,128)(2,1)S(1)}, f32[512,2,128]{2,1,0:T(2,128)S(1)}) fusion(bf16[512,2,128]{2,1,0:T(2,128)(2,1)} %param.10, bf16[512,2,128]{2,1,0:T(2,128)(2,1)} %param.9), kind=kLoop, calls=%fused_computation.33 | loop fusion | flops 1048576 | bytes 1310720 | tf_op jit(solution)/shard_map/transpose | solution.py:439
  3.0 0.2 copy.10
  3.1 0.7 fusion.20.hid_ref
  3.9 153.5 %shard_map.93 = (bf16[48,8192]{1,0:T(8,128)(2,1)}, bf16[48,8192]{1,0:T(8,128)(2,1)}, f32[2,512,256]{2,1,0:T(8,128)}) custom-call(bf16[16,1536]{1,0:T(8,128)(2,1)} %bitcast.23, bf16[3072,128]{1,0:T(8,128)(2,1)} %bitcast.22, bf16[272,512]{1,0:T(8,128)(2,1)} %fusion.20.hid_ref), custom_call_target="tpu_custom_call" | custom-call | tf_op jit(solution)/shard_map/pallas_call | solution.py:390
  157.4 0.0 copy-start
  157.4 0.0 copy-start.1
  157.5 1.3 slice_add_fusion
  158.8 0.0 copy-start.2
  158.8 0.3 add.25
  159.1 0.0 copy-done
  159.1 0.0 copy-done.1
  159.1 0.0 copy-start.3
  159.1 0.0 copy-start.4
  159.1 1.6 fusion.19
  160.7 0.0 copy-done.2
  160.7 0.0 copy-done.3
  160.7 0.0 copy-done.4
  160.7 2.1 %fusion.6 = (bf16[1,48,8192]{2,1,0:T(8,128)(2,1)}, f32[1,48,8192]{2,1,0:T(8,128)}) fusion(bf16[1,48,8192]{2,1,0:T(8,128)(2,1)S(1)} %copy-done.2, bf16[48,8192]{1,0:T(8,128)(2,1)S(1)} %copy-done.4, bf16[48,8192]{1,0:T(8,128)(2,1)S(1)} %copy-done.3), kind=kLoop, calls=%fused_computation.10 | loop fusion | flops 5505024 | bytes 4718592 | tf_op jit(solution)/shard_map/convert_element_type | solution.py:453
Async XLA Ops:
  157.4 1.6 %copy-start = (bf16[512,2,128]{2,1,0:T(2,128)(2,1)S(1)}, bf16[512,2,128]{2,1,0:T(2,128)(2,1)}, u32[]{:S(2)}) copy-start(bf16[512,2,128]{2,1,0:T(2,128)(2,1)} %param.10) | copy-start | bytes 786436
  157.4 1.6 %copy-start.1 = (bf16[512,2,128]{2,1,0:T(2,128)(2,1)S(1)}, bf16[512,2,128]{2,1,0:T(2,128)(2,1)}, u32[]{:S(2)}) copy-start(bf16[512,2,128]{2,1,0:T(2,128)(2,1)} %param.9) | copy-start | bytes 786436
  158.8 1.9 %copy-start.2 = (bf16[1,48,8192]{2,1,0:T(8,128)(2,1)S(1)}, bf16[1,48,8192]{2,1,0:T(8,128)(2,1)}, u32[]{:S(2)}) copy-start(bf16[1,48,8192]{2,1,0:T(8,128)(2,1)} %param.13) | copy-start | bytes 2359300
  159.1 1.6 copy-start.3
  159.1 1.6 copy-start.4

commit v4 on v3

--- a/solution.py
+++ b/solution.py
@@ -23,9 +23,10 @@
 
 
 def kernel(
-    og_ref, w_ref, hid_ref, wr_ref, gr_ref, dr_ref,
-    xb, x2, wp, ht, htq, mk, dn, ds, gf, gx, gy, gu, px, py, gst,
+    og_ref, w_ref, gate_ref, up_ref, named_ref, wr_ref, gr_ref, dr_ref, da_ref,
+    xb, x2, wp, hf, ht, htq, mk, dn, ds, gf, gx, gy, gu, px, py, gst,
     zs, zr, ags, agr, ws, wr, hs, hr, dsend, drecv, xs, xr, ps, pr, gs, grs, was, war,
+    row_sem, plane_sem,
 ):
     half = og_ref.shape[1]
     cols = w_ref.shape[1]
@@ -65,35 +66,25 @@
 
     barrier = pltpu.get_barrier_semaphore()
 
-    def greet(device):
+    def greet(semaphore, device):
         pl.semaphore_signal(
-            barrier, inc=1, device_id=device, device_id_type=pl.DeviceIdType.MESH
+            semaphore, inc=1, device_id=device, device_id_type=pl.DeviceIdType.MESH
         )
 
-    for device in (z_up, z_down, other, at_lo(beside), at_lo(across)):
-        greet(device)
-
-    def greet_cells(i, carry):
-        c = (cell + i) % CELLS
-        greet(owner(z_lo, toward, c))
-        greet(owner(beside, away, c))
-        greet(owner(beside, far, c))
-        return carry
-
-    def greet_near(i, carry):
-        greet(owner(z_lo, z_hi, (cell + i) % CELLS))
-        return carry
-
-    lax.fori_loop(0, CELLS, greet_cells, 0)
-    lax.fori_loop(1, CELLS, greet_near, 0)
+    column = [at_cell(x, (y + i) % NY) for i in range(1, NY)]
+    levels = [owner(z_lo, (z_hi + i) % NHI, cell) for i in range(1, NHI)]
+    levels += [owner(beside, (z_hi + i) % NHI, cell) for i in range(NHI)]
+    nearby = [z_up, z_down, other, at_lo(across)]
+    nearby += [at_cell((x + i) % NX, y) for i in range(1, NX)] + column + levels
+    for device in nearby:
+        greet(barrier, device)
 
     def expert_lanes(s, c):
         return pl.ds(pl.multiple_of((s * 2 + c) * cols, cols), cols)
 
     xb[OWN, x, y] = og_ref[...]
     wp[:, expert_lanes(side, core)] = w_ref[...]
-    ht[0] = hid_ref[...]
-    pl.semaphore_wait(barrier, 5 + NHI * CELLS - 1)
+    pl.semaphore_wait(barrier, len(nearby))
 
     def z_copy(q, step):
         device = z_down if step > 0 else z_up
@@ -123,8 +114,10 @@
     from_beside = wp.at[:, expert_lanes(1 - side, core)]
     relay = remote(from_beside, from_beside, was.at[2], war.at[2], other)
     start(to_core)
-
-    hidden_copy = remote(hid_ref, ht.at[1], hs.at[0], hr.at[0], at_lo(across))
+    for device in column:
+        greet(row_sem, device)
+
+    hidden_copy = remote(ht.at[0], ht.at[1], hs.at[0], hr.at[0], at_lo(across))
 
     part = half // 2
     piece = part // 2
@@ -197,7 +190,7 @@
         lax.fori_loop(1, CELLS, send_near, 0)
 
     block = CELLS * 8
-    tokens = dr_ref.shape[1]
+    tokens = named_ref.shape[1]
 
     def token_lane(q):
         return pl.multiple_of(((z + 2 * (q + SLOTS - OWN)) % NZ) // NLO * block, block)
@@ -230,11 +223,11 @@
         return carry
 
     def dh_copy(q):
-        src = ds.at[pl.ds(q * block, block), :]
-        lane = token_lane(q)
+        src = ds.at[pl.ds(q * 2 * block, 2 * block), :]
+        row = pl.multiple_of(2 * token_lane(q), 2 * block)
         if (q - OWN) % 2 == 0:
-            return pltpu.make_async_copy(src, dr_ref.at[0, pl.ds(lane, block), :], drecv.at[0])
-        return remote(src, dr_ref.at[1, pl.ds(lane, block), :], dsend.at[q], drecv.at[0], at_lo(across))
+            return pltpu.make_async_copy(src, dr_ref.at[pl.ds(row, 2 * block), :], drecv.at[0])
+        return remote(src, da_ref.at[pl.ds(row, 2 * block), :], dsend.at[q], drecv.at[1], at_lo(across))
 
     def backward(r):
         first, slots = RANGES[r]
@@ -248,8 +241,17 @@
                 picked = mk[q, k, 0] * dn[at, 0:cols]
                 for e in range(1, PAIR):
                     picked += mk[q, k, e] * dn[at, e * cols:(e + 1) * cols]
-                ds[at, k * cols:(k + 1) * cols] = picked
-
+                ds[pl.ds(q * 2 * block + k, block, stride=2), :] = picked
+
+    gate = gate_ref[...].astype(F32)
+    hf[...] = gate * jax.nn.sigmoid(gate) * up_ref[...].astype(F32)
+    for k in range(2):
+        ht[0, k * cols:(k + 1) * cols, :] = hf[pl.ds(k, tokens, stride=2), :].T.astype(BF16)
+    ht[0, 2 * cols:2 * cols + 16, :] = named_ref[...]
+
+    pl.semaphore_wait(row_sem, len(column))
+    for device in levels:
+        greet(plane_sem, device)
     z_step(1)
     z_step(2)
     direct(0, 0)
@@ -260,6 +262,7 @@
     direct(2, 0)
     start(to_beside)
     start(hidden_copy)
+    pl.semaphore_wait(plane_sem, len(levels))
     send_weights()
     turn(0)
     forward(1, 0)
@@ -372,13 +375,14 @@
     pltpu.make_async_copy(sent, sent, gs.at[0]).wait()
     pltpu.make_async_copy(wr_ref, wr_ref, wr.at[0]).wait()
     pltpu.make_async_copy(dr_ref, dr_ref, drecv.at[0]).wait()
+    pltpu.make_async_copy(da_ref, da_ref, drecv.at[1]).wait()
     pltpu.make_async_copy(gr_ref, gr_ref, grs.at[0]).wait()
 
 
-def exchange_all(og, weight, hidden):
+def exchange_all(og, weight, gate, up, named):
     half = og.shape[1]
     width, cols = weight.shape
-    tokens = hidden.shape[1]
+    tokens = named.shape[1]
     rows = width // (NHI * CELLS)
     ff = cols * NHI * CELLS
     total = SLOTS * CELLS * 8
@@ -392,19 +396,21 @@
         out_shape=(
             jax.ShapeDtypeStruct((rows, ff), BF16),
             jax.ShapeDtypeStruct((rows, ff), BF16),
-            jax.ShapeDtypeStruct((2, tokens, 2 * cols), F32),
+            jax.ShapeDtypeStruct((2 * tokens, cols), F32),
+            jax.ShapeDtypeStruct((2 * tokens, cols), F32),
         ),
-        in_specs=[vmem] * 3,
-        out_specs=(any_space,) * 3,
+        in_specs=[vmem] * 5,
+        out_specs=(any_space,) * 4,
         scratch_shapes=[
             pltpu.VMEM((SLOTS, NX, NY, 16, half), BF16),
             pltpu.VMEM((total, width), BF16),
             pltpu.VMEM((width, PAIR * cols), BF16),
+            pltpu.VMEM((2 * tokens, cols), F32),
             pltpu.VMEM((2, 2 * cols + 16, tokens), BF16),
             pltpu.VMEM((PAIR * cols, total), BF16),
             pltpu.VMEM((SLOTS, 2, PAIR, CELLS * 8, cols), F32),
             pltpu.VMEM((total, PAIR * cols), F32),
-            pltpu.VMEM((total, 2 * cols), F32),
+            pltpu.VMEM((2 * total, cols), F32),
             pltpu.VMEM((NHI, PAIR * cols, piece), F32),
             pltpu.VMEM((NHI, 2, cols, piece), BF16),
             pltpu.VMEM((NHI, 2, cols, piece), BF16),
@@ -416,16 +422,17 @@
             dma((ranges, 2, 2, 4)), dma((ranges, 2, 2, 4)),
             dma((1,)), dma((1,)),
             dma((1,)), dma((1,)),
-            dma((SLOTS,)), dma((1,)),
+            dma((SLOTS,)), dma((2,)),
             dma((NHI,)), dma((NHI,)),
             dma((NHI,)), dma((NHI,)),
             dma((1,)), dma((1,)),
             dma((3,)), dma((3,)),
+            pltpu.SemaphoreType.REGULAR, pltpu.SemaphoreType.REGULAR,
         ],
         compiler_params=pltpu.CompilerParams(
             collective_id=0, has_side_effects=True, vmem_limit_bytes=56 * 1024 * 1024
         ),
-    )(og, weight, hidden)
+    )(og, weight, gate, up, named)
 
 
 def body(out_grad, gate_saved, up_saved, routing, down_weight, momentum):
@@ -436,11 +443,12 @@
     gate = gate_saved.astype(F32)
     up = up_saved.astype(F32)
     sigma = jax.nn.sigmoid(gate)
-    hidden = (gate * sigma * up).astype(BF16).transpose(1, 2, 0)
-    named = jnp.zeros((16, group_tok), BF16).at[:topk].set(routing.T.astype(BF16))
-    sent = jnp.concatenate([hidden.reshape(topk * cols, group_tok), named], axis=0)
-    shard_weight, shard_grad, back = exchange_all(og, down_weight[0], sent)
-    dh = (back[0] + back[1]).reshape(group_tok, topk, cols)
+    named = jnp.pad(routing.T.astype(BF16), ((0, 16 - topk), (0, 0)))
+    flat = (group_tok * topk, cols)
+    shard_weight, shard_grad, near, across = exchange_all(
+        og, down_weight[0], gate_saved.reshape(flat), up_saved.reshape(flat), named
+    )
+    dh = near.reshape(gate.shape) + across.reshape(gate.shape)
     d_up = (dh * gate * sigma).astype(BF16)
     d_gate = (dh * up * sigma * (1.0 + gate * (1.0 - sigma))).astype(BF16)
 

time: 163 us -> 159 us (0.975)
  Pallas kernels: 154 us -> 151 us
  other arithmetic: 8.13 us -> 6.17 us
    pallas_call x1, Pallas kernels: 154 us -> 151 us  [exchange_all(): pl.pallas_call(kernel, out_shape=(jax.ShapeDtypeStruct((rows, ff), BF16),...]
    transpose x1 -> x0, other arithmetic: 1.65 us -> none  [body(): hidden = (gate * sigma * up).astype(BF16).transpose(1, 2, 0)]
where the time goes in v4:
time: 159 us
  Pallas kernels  151 us (95%)
  other arithmetic  6.17 us (4%)
    pallas_call x1, Pallas kernels, exchange_all(): pl.pallas_call(kernel, out_shape=(jax.ShapeDtypeStruct((rows, ff), BF16),...  151 us

profile of v4, /device:TPU:32, one launch (start us, length us, event | category | flops | bytes accessed | tf_op | source)
XLA Modules:
  0.0 158.6 jit_solution(10685730941056831134)
XLA Ops:
  0.6 0.0 copy-start.1
  0.6 0.0 copy-start
  0.7 0.7 convert_bitcast_fusion
  1.4 0.6 pad.4.named_ref
  2.0 151.0 %shard_map.93 = (bf16[48,8192]{1,0:T(8,128)(2,1)}, bf16[48,8192]{1,0:T(8,128)(2,1)}, f32[1024,128]{1,0:T(8,128)}, f32[1024,128]{1,0:T(8,128)}) custom-call(bf16[16,1536]{1,0:T(8,128)(2,1)} %bitcast.25, bf16[3072,128]{1,0:T(8,128)(2,1)} %bitcast.24, bf16[1024,128]{1,0:T(8,128)(2,1)} %bitcast.22, bf16[1024,128]{1,0:T(8,128)(2,1)} %bitcast.23, ...), custom_call_target="tpu_custom_call" | custom-call | tf_op jit(solution)/shard_map/pallas_call | solution.py:394
  153.1 0.0 copy-start.2
  153.1 0.0 copy-start.3
  153.1 0.0 copy-start.4
  153.1 1.4 add.20
  154.5 0.0 copy-done.1
  154.5 0.0 copy-done
  154.5 1.9 %fusion.16 = (bf16[512,2,128]{2,1,0:T(2,128)(2,1)}, bf16[512,2,128]{2,1,0:T(2,128)(2,1)}) fusion(f32[512,2,128]{2,1,0:T(2,128)S(1)} %bitcast.21, bf16[512,2,128]{2,1,0:T(2,128)(2,1)S(1)} %copy-done, bf16[512,2,128]{2,1,0:T(2,128)(2,1)S(1)} %copy-done.1), kind=kLoop, calls=%fused_computation.23 | loop fusion | flops 1966080 | bytes 1572864 | tf_op jit(solution)/shard_map/convert_element_type | solution.py:452
  156.4 0.0 copy-done.2
  156.4 0.0 copy-done.3
  156.4 0.0 copy-done.4
  156.4 2.1 %fusion.6 = (bf16[1,48,8192]{2,1,0:T(8,128)(2,1)}, f32[1,48,8192]{2,1,0:T(8,128)}) fusion(bf16[1,48,8192]{2,1,0:T(8,128)(2,1)S(1)} %copy-done.2, bf16[48,8192]{1,0:T(8,128)(2,1)S(1)} %copy-done.4, bf16[48,8192]{1,0:T(8,128)(2,1)S(1)} %copy-done.3), kind=kLoop, calls=%fused_computation.10 | loop fusion | flops 5505024 | bytes 4718592 | tf_op jit(solution)/shard_map/convert_element_type | solution.py:461
Async XLA Ops:
  0.6 153.9 %copy-start.1 = (bf16[512,2,128]{2,1,0:T(2,128)(2,1)S(1)}, bf16[512,2,128]{2,1,0:T(2,128)(2,1)}, u32[]{:S(2)}) copy-start(bf16[512,2,128]{2,1,0:T(2,128)(2,1)} %param.8) | copy-start | bytes 786436
  0.6 153.9 %copy-start = (bf16[512,2,128]{2,1,0:T(2,128)(2,1)S(1)}, bf16[512,2,128]{2,1,0:T(2,128)(2,1)}, u32[]{:S(2)}) copy-start(bf16[512,2,128]{2,1,0:T(2,128)(2,1)} %param.7) | copy-start | bytes 786436
  153.1 3.3 %copy-start.2 = (bf16[1,48,8192]{2,1,0:T(8,128)(2,1)S(1)}, bf16[1,48,8192]{2,1,0:T(8,128)(2,1)}, u32[]{:S(2)}) copy-start(bf16[1,48,8192]{2,1,0:T(8,128)(2,1)} %param.11) | copy-start | bytes 2359300
  153.1 3.3 %copy-start.3 = (bf16[48,8192]{1,0:T(8,128)(2,1)S(1)}, bf16[48,8192]{1,0:T(8,128)(2,1)}, u32[]{:S(2)}) copy-start(bf16[48,8192]{1,0:T(8,128)(2,1)} %get-tuple-element.10) | copy-start | bytes 2359300
  153.1 3.3 %copy-start.4 = (bf16[48,8192]{1,0:T(8,128)(2,1)S(1)}, bf16[48,8192]{1,0:T(8,128)(2,1)}, u32[]{:S(2)}) copy-start(bf16[48,8192]{1,0:T(8,128)(2,1)} %get-tuple-element.11) | copy-start | bytes 2359300

commit v5 on v4

--- a/solution.py
+++ b/solution.py
@@ -256,12 +256,12 @@
     z_step(2)
     direct(0, 0)
     z_step(3)
+    start(to_beside)
+    start(hidden_copy)
     direct(1, 0)
     forward(0, 0)
     z_step(4)
     direct(2, 0)
-    start(to_beside)
-    start(hidden_copy)
     pl.semaphore_wait(plane_sem, len(levels))
     send_weights()
     turn(0)

time: 159 us -> 156 us (0.981)
  Pallas kernels: 151 us -> 148 us
    pallas_call x1, Pallas kernels: 151 us -> 148 us  [exchange_all(): pl.pallas_call(kernel, out_shape=(jax.ShapeDtypeStruct((rows, ff), BF16),...]
where the time goes in v5:
time: 156 us; the launch traced here: 155 us
  Pallas kernels  148 us (95%)
  other arithmetic  6.17 us (4%)
    pallas_call x1, Pallas kernels, exchange_all(): pl.pallas_call(kernel, out_shape=(jax.ShapeDtypeStruct((rows, ff), BF16),...  148 us

profile of v5, /device:TPU:32, one launch (start us, length us, event | category | flops | bytes accessed | tf_op | source)
XLA Modules:
  0.0 155.4 jit_solution(16642989871461881587)
XLA Ops:
  0.6 0.0 copy-start.1
  0.6 0.0 copy-start
  0.7 0.7 convert_bitcast_fusion
  1.4 0.6 pad.4.named_ref
  2.0 147.9 %shard_map.93 = (bf16[48,8192]{1,0:T(8,128)(2,1)}, bf16[48,8192]{1,0:T(8,128)(2,1)}, f32[1024,128]{1,0:T(8,128)}, f32[1024,128]{1,0:T(8,128)}) custom-call(bf16[16,1536]{1,0:T(8,128)(2,1)} %bitcast.25, bf16[3072,128]{1,0:T(8,128)(2,1)} %bitcast.24, bf16[1024,128]{1,0:T(8,128)(2,1)} %bitcast.22, bf16[1024,128]{1,0:T(8,128)(2,1)} %bitcast.23, ...), custom_call_target="tpu_custom_call" | custom-call | tf_op jit(solution)/shard_map/pallas_call | solution.py:394
  149.9 0.0 copy-start.2
  149.9 0.0 copy-start.3
  149.9 0.0 copy-start.4
  149.9 1.4 add.20
  151.3 0.0 copy-done.1
  151.3 0.0 copy-done
  151.3 1.9 %fusion.16 = (bf16[512,2,128]{2,1,0:T(2,128)(2,1)}, bf16[512,2,128]{2,1,0:T(2,128)(2,1)}) fusion(f32[512,2,128]{2,1,0:T(2,128)S(1)} %bitcast.21, bf16[512,2,128]{2,1,0:T(2,128)(2,1)S(1)} %copy-done, bf16[512,2,128]{2,1,0:T(2,128)(2,1)S(1)} %copy-done.1), kind=kLoop, calls=%fused_computation.23 | loop fusion | flops 1966080 | bytes 1572864 | tf_op jit(solution)/shard_map/convert_element_type | solution.py:452
  153.2 0.0 copy-done.2
  153.2 0.0 copy-done.3
  153.2 0.0 copy-done.4
  153.2 2.1 %fusion.6 = (bf16[1,48,8192]{2,1,0:T(8,128)(2,1)}, f32[1,48,8192]{2,1,0:T(8,128)}) fusion(bf16[1,48,8192]{2,1,0:T(8,128)(2,1)S(1)} %copy-done.2, bf16[48,8192]{1,0:T(8,128)(2,1)S(1)} %copy-done.4, bf16[48,8192]{1,0:T(8,128)(2,1)S(1)} %copy-done.3), kind=kLoop, calls=%fused_computation.10 | loop fusion | flops 5505024 | bytes 4718592 | tf_op jit(solution)/shard_map/convert_element_type | solution.py:461
Async XLA Ops:
  0.6 150.7 %copy-start.1 = (bf16[512,2,128]{2,1,0:T(2,128)(2,1)S(1)}, bf16[512,2,128]{2,1,0:T(2,128)(2,1)}, u32[]{:S(2)}) copy-start(bf16[512,2,128]{2,1,0:T(2,128)(2,1)} %param.8) | copy-start | bytes 786436
  0.6 150.7 %copy-start = (bf16[512,2,128]{2,1,0:T(2,128)(2,1)S(1)}, bf16[512,2,128]{2,1,0:T(2,128)(2,1)}, u32[]{:S(2)}) copy-start(bf16[512,2,128]{2,1,0:T(2,128)(2,1)} %param.7) | copy-start | bytes 786436
  149.9 3.3 %copy-start.2 = (bf16[1,48,8192]{2,1,0:T(8,128)(2,1)S(1)}, bf16[1,48,8192]{2,1,0:T(8,128)(2,1)}, u32[]{:S(2)}) copy-start(bf16[1,48,8192]{2,1,0:T(8,128)(2,1)} %param.11) | copy-start | bytes 2359300
  149.9 3.3 %copy-start.3 = (bf16[48,8192]{1,0:T(8,128)(2,1)S(1)}, bf16[48,8192]{1,0:T(8,128)(2,1)}, u32[]{:S(2)}) copy-start(bf16[48,8192]{1,0:T(8,128)(2,1)} %get-tuple-element.10) | copy-start | bytes 2359300
  149.9 3.3 %copy-start.4 = (bf16[48,8192]{1,0:T(8,128)(2,1)S(1)}, bf16[48,8192]{1,0:T(8,128)(2,1)}, u32[]{:S(2)}) copy-start(bf16[48,8192]{1,0:T(8,128)(2,1)} %get-tuple-element.11) | copy-start | bytes 2359300
